TPU v7x, 512 devices: a whole 4x8x8 slice. The times are simulated.
512 devices in a mesh: frame: 64 (over z, x, core), head: 8 (over y).
Axes of the slice: x: 4, y: 8, z: 8, core: 2. Of those that a mesh axis runs over, the one named last changes fastest.
Arguments:
- queries: bfloat16 [32768, 3072], P(('frame', 'head')), may hold values from -80 to 80
- keys: bfloat16 [32768, 3072], P(('frame', 'head')), may hold values from -80 to 80
- values: bfloat16 [32768, 3072], P(('frame', 'head')), may hold values from -6 to 6
- q_gain: float32 [3072], replicated, may hold values from 0.5 to 2
- k_gain: float32 [3072], replicated, may hold values from 0.5 to 2
- block_offset: int32 [64, 3, 2], replicated, may hold values from 0 to 3, as said below
Outputs:
- attended: bfloat16 [32768, 3072], P(('frame', 'head'))
Inputs may be any that keep to these rules, and one draw needn't show every extreme that they name: block_offset[f, l, s] is below 2 ** l.
All inputs are finite; a program needn't handle non-finite values.
Results may differ from a plain program's by a relative error of at most 0.012.
The roundings to bfloat16 on the way count: a program that leaves them out, or rounds other values in their place, can miss the bound.
Values may be sent and summed in bfloat16 or wider, within the bound.
No kernel may reach another device: no remote copies, remote signals or barrier semaphores. Data moves between devices by JAX's collectives and lax.ppermute only.
A program may use at most 128 MiB of HBM per device.

v0:
```python
import math

import jax
import jax.numpy as jnp
from jax import lax
from jax.experimental import pallas as pl
from jax.experimental.pallas import tpu as pltpu
from jax.sharding import Mesh
from jax.sharding import PartitionSpec as P

HD = 128
HEADS = 24
TOK = 64
SLOTS = 32
LOG2E = 1.4426950408889634
FACTOR = LOG2E / math.sqrt(HD)
VMEM_LIMIT = 48 * 1024 * 1024
WHOLE = pl.BlockSpec(memory_space=pltpu.VMEM)
TABLE = pl.BlockSpec(memory_space=pltpu.SMEM)
ANYWHERE = pl.BlockSpec(memory_space=pl.ANY)


THEIRS = 13
ZERO = 25
OWN_FLOPS = 40 * 8704 * 512 * HD
FRAMES = 26
DISTANCES = (0, 1, -1, 2, -2, 3, -3, 4, -4, 6, -6, 5, -5, 7, -7)


def normed(x_ref, gain_ref):
    x = x_ref[...].astype(jnp.float32)
    mean_square = jnp.mean(x * x, axis=-1, keepdims=True)
    return (x * lax.rsqrt(mean_square + 1e-06) * gain_ref[...]).astype(jnp.bfloat16)


def spread(x, out_ref):
    for h in range(HEADS):
        out_ref[h] = x[:, h * HD : (h + 1) * HD]
    for h in range(HEADS, SLOTS):
        out_ref[h] = jnp.zeros(out_ref.shape[1:], out_ref.dtype)


def prepare_kv(k_ref, v_ref, gain_ref, out_ref):
    spread(normed(k_ref, gain_ref), out_ref.at[:, 0])
    spread(v_ref, out_ref.at[:, 1])


def prepare_q(q_ref, gain_ref, out_ref):
    spread(normed(q_ref, gain_ref), out_ref)


def lane_fold(op, matrix):
    parts = [matrix[:, n : n + HD] for n in range(0, matrix.shape[1], HD)]
    while len(parts) > 1:
        parts = [op(*parts[n : n + 2]) if n + 1 < len(parts) else parts[n] for n in range(0, len(parts), 2)]
    return parts[0]


def width(d):
    return 512 if abs(d) <= 1 else 256 if abs(d) <= 3 else 128


def place(i, d):
    if d % 2 == 0:
        n = 4 + i + d // 2
        return n, "low" if n < 4 else "high" if n >= 8 else None
    n = 4 + i + (d - 1) // 2
    return THEIRS + n, "low" if n < 3 else "edge_low" if n == 3 else "high" if n >= 8 else "edge_high" if n == 7 else None


class Unit:
    def __init__(self, meta_ref, i, parity, inside, keys, values):
        self.i = i
        self.parity = parity
        self.offs = [[meta_ref[2 + (i * 3 + level) * 2 + side] for side in range(2)] for level in range(3)]
        self.keys = keys
        self.values = values
        used = [d for d in DISTANCES if (place(i, d)[1] is None) == inside]
        self.both = []
        self.far = []
        for size, groups in ((512, self.both), (256, self.both), (128, self.far)):
            here = [d for d in used if width(d) == size]
            per = 512 // size
            groups += [here[n : n + per] for n in range(0, len(here), per)]

    def q(self, q_ref, high):
        return q_ref[self.i, :, high, self.parity].reshape(HD, HD)

    def gather(self, fetch, group, cls):
        parts = []
        for d in group:
            side = 0 if d < 0 else 1
            if abs(d) <= 1:
                at = (slice(None),) * 3
            elif abs(d) <= 3:
                at = (slice(None), slice(None), (cls + self.offs[1][side]) & 1)
            else:
                kept = (cls + self.offs[2][side]) & 3
                at = (slice(None), kept >> 1, kept & 1)
            parts.append(fetch(self.i, d, at).reshape(width(d), HD))
        return jnp.concatenate(parts, axis=0)


def score(unit, q_ref, s_ref, before=None):
    q = [unit.q(q_ref, high) for high in range(2)]
    both = jnp.concatenate(q, axis=0)
    contract = (((1,), (1,)), ((), ()))
    top = before
    start = 0
    for group in unit.both:
        key = unit.gather(unit.keys, group, unit.parity)
        s = lax.dot_general(both, key, contract, preferred_element_type=jnp.float32)
        s_ref[:, start : start + key.shape[0]] = s
        start += key.shape[0]
        part = lane_fold(jnp.maximum, s)
        top = part if top is None else jnp.maximum(top, part)
    tops = []
    for high in range(2):
        rows = slice(high * HD, (high + 1) * HD)
        own = top[rows]
        at = start
        for group in unit.far:
            key = unit.gather(unit.keys, group, unit.parity + 2 * high)
            s = lax.dot_general(q[high], key, contract, preferred_element_type=jnp.float32)
            s_ref[rows, at : at + key.shape[0]] = s
            at += key.shape[0]
            own = jnp.maximum(own, lane_fold(jnp.maximum, s))
        tops.append(jnp.max(own, axis=1, keepdims=True))
    return tops


def mix(unit, tops, s_ref, flags):
    shift = jnp.concatenate(tops, axis=0) * FACTOR
    sums = {}

    def weigh(rows, start, group, moved):
        size = width(group[0])
        weights = jnp.exp2(s_ref[rows, start : start + size * len(group)] * FACTOR - moved)
        for m, d in enumerate(group):
            part = lane_fold(jnp.add, weights[:, m * size : (m + 1) * size])
            key = (place(unit.i, d)[1], rows.start, rows.stop)
            sums[key] = sums[key] + part if key in sums else part
        return weights.astype(jnp.bfloat16)

    total = None
    start = 0
    for group in unit.both:
        w = weigh(slice(0, 256), start, group, shift)
        start += w.shape[1]
        mixed = jnp.dot(w, unit.gather(unit.values, group, unit.parity), preferred_element_type=jnp.float32)
        total = mixed if total is None else total + mixed
    result = []
    for high in range(2):
        rows = slice(high * HD, (high + 1) * HD)
        own = total[rows]
        at = start
        for group in unit.far:
            w = weigh(rows, at, group, shift[rows])
            at += w.shape[1]
            value = unit.gather(unit.values, group, unit.parity + 2 * high)
            own = own + jnp.dot(w, value, preferred_element_type=jnp.float32)
        lanes = None
        for (kind, first, last), part in sums.items():
            if not first <= rows.start < last:
                continue
            if last - first == 256:
                part = part[rows]
            if kind is not None:
                part = part * flags[kind]
            lanes = part if lanes is None else lanes + part
        result.append((lanes, own))
    return result


def attend_own(meta_ref, q_ref, mine_ref, theirs_ref, top_ref, lanes_ref, total_ref, s_even, s_odd):
    core = meta_ref[1]

    def fetch(which):
        def of(i, d, at):
            n = place(i, d)[0]
            ref, n = (mine_ref, n - 4) if d % 2 == 0 else (theirs_ref, n - THEIRS - 4 + core)
            return ref[(n,) + at + (which,)]

        return of

    units = [Unit(meta_ref, i, parity, True, fetch(0), fetch(1)) for i in range(4) for parity in range(2)]
    s_refs = (s_even, s_odd)
    tops = score(units[0], q_ref, s_refs[0])
    for n, unit in enumerate(units):
        now = tops
        if n + 1 < len(units):
            tops = score(units[n + 1], q_ref, s_refs[(n + 1) % 2])
        for high, (lanes, own) in enumerate(mix(unit, now, s_refs[n % 2], None)):
            rows = slice(high * HD, (high + 1) * HD)
            top_ref[n, rows] = jnp.broadcast_to(now[high], (HD, HD))
            lanes_ref[n, rows] = lanes
            total_ref[n, rows] = own


def attend_rest(
    meta_ref, q_ref, top_ref, lanes_ref, total_ref, own, low, high_ref, their_own, their_low, their_high,
    out_ref, k_ref, v_ref, s_even, s_odd, sems,
):
    z = meta_ref[0]
    core = meta_ref[1]
    sources = ((low, 0), (high_ref, 8), (their_low, THEIRS - core), (their_own, THEIRS - core + 4),
               (their_high, THEIRS - core + 8))

    def copy(src, which, ref, slot, n):
        made = pltpu.make_async_copy(src.at[:, :, :, :, which], ref.at[pl.ds(slot, 4)], sems.at[n])
        made.start()
        return made

    k_copies = [copy(src, 0, k_ref, slot, n) for n, (src, slot) in enumerate(sources + ((own, 4),))]
    v_copies = [copy(src, 1, v_ref, slot, n + 6) for n, (src, slot) in enumerate(sources)]
    v_ref[ZERO] = jnp.zeros(v_ref.shape[1:], v_ref.dtype)
    flag = lambda cond: jnp.where(cond, 1.0, 0.0).astype(jnp.float32)
    flags = {
        "low": flag(z > 0),
        "edge_low": flag((z > 0) | (core == 1)),
        "edge_high": flag((z < 7) | (core == 0)),
        "high": flag(z < 7),
    }

    def slot(i, d, outside):
        n, kind = place(i, d)
        return jnp.where(flags[kind] > 0, n, outside)

    def keys(i, d, at):
        return k_ref[(slot(i, d, 4 + i),) + at]

    def values(i, d, at):
        return v_ref[(slot(i, d, ZERO),) + at]

    units = [Unit(meta_ref, i, parity, False, keys, values) for i in range(4) for parity in range(2)]
    s_refs = (s_even, s_odd)
    for made in k_copies:
        made.wait()
    tops = score(units[0], q_ref, s_refs[0], top_ref[0])
    for made in v_copies:
        made.wait()
    for n, unit in enumerate(units):
        now = tops
        if n + 1 < len(units):
            tops = score(units[n + 1], q_ref, s_refs[(n + 1) % 2], top_ref[n + 1])
        for high, (lanes, mixed) in enumerate(mix(unit, now, s_refs[n % 2], flags)):
            rows = slice(high * HD, (high + 1) * HD)
            carried = jnp.exp2((top_ref[n, rows] - now[high]) * FACTOR)
            lanes = lanes + lanes_ref[n, rows] * carried
            mixed = mixed + total_ref[n, rows] * carried
            row_sum = jnp.sum(lanes, axis=1, keepdims=True)
            out_ref[unit.i, :, high, unit.parity] = (mixed / row_sum).astype(jnp.bfloat16).reshape(2, TOK, HD)


def side_by_side(x_ref, out_ref):
    for h in range(HEADS):
        out_ref[:, h * HD : (h + 1) * HD] = x_ref[h]


def call(kernel, out_shape, specs, flops=0, scratch=(), **more):
    params = pltpu.CompilerParams(vmem_limit_bytes=VMEM_LIMIT)
    cost = pl.CostEstimate(flops=flops, bytes_accessed=4 << 20, transcendentals=flops // 512)
    return pl.pallas_call(
        kernel, out_shape=out_shape, in_specs=specs, scratch_shapes=scratch,
        compiler_params=params, cost_estimate=cost, **more,
    )


def exchange(x):
    return lax.all_to_all(x, ("x", "y"), split_axis=0, concat_axis=0, tiled=True)


def local(queries, keys, values, q_gain, k_gain, block_offset):
    half = jnp.bfloat16
    z = lax.axis_index("z")
    core = lax.axis_index("c")
    frame = lax.dynamic_slice_in_dim(block_offset.reshape(8, 4, 2, 6), z, 1, 0)
    table = lax.dynamic_slice_in_dim(frame, core, 1, 2).reshape(24)
    meta = jnp.concatenate([jnp.stack([z, core]).astype(jnp.int32), table])

    kv = call(prepare_kv, jax.ShapeDtypeStruct((SLOTS, 2, TOK, HD), half), [WHOLE] * 3)(
        keys, values, k_gain.reshape(1, -1)
    )
    queries, kv = lax.optimization_barrier((queries, kv))
    q = call(prepare_q, jax.ShapeDtypeStruct((SLOTS, TOK, HD), half), [WHOLE] * 2)(queries, q_gain.reshape(1, -1))
    kv = exchange(kv)
    q, kv = lax.optimization_barrier((q, kv))
    blocks = (4, 2, 2, 2, TOK, HD)
    q = exchange(q).reshape(blocks)

    mine = kv.reshape(4, 2, 2, 2, 2, TOK, HD)
    swap = [(0, 1), (1, 0)]
    low = lax.ppermute(mine, "z", [(n, n + 1) for n in range(7)])
    high = lax.ppermute(mine, "z", [(n + 1, n) for n in range(7)])
    theirs = lax.ppermute(mine, "c", swap)
    their_low = lax.ppermute(low, "c", swap)
    their_high = lax.ppermute(high, "c", swap)

    scores = [pltpu.VMEM((256, 2560), jnp.float32)] * 2
    state = [jax.ShapeDtypeStruct((8, 256, HD), jnp.float32)] * 3
    state = call(attend_own, state, [TABLE] + [WHOLE] * 3, flops=OWN_FLOPS, scratch=scores)(meta, q, mine, theirs)
    kept = pltpu.VMEM((FRAMES, 2, 2, 2, TOK, HD), half)
    out = call(
        attend_rest,
        jax.ShapeDtypeStruct(blocks, half),
        [TABLE] + [WHOLE] * 4 + [ANYWHERE] * 6,
        flops=4 * 5632 * 512 * HD,
        scratch=[kept, kept] + scores + [pltpu.SemaphoreType.DMA((11,))],
    )(meta, q, *state, mine, low, high, theirs, their_low, their_high)
    back = exchange(out.reshape(SLOTS, TOK, HD))
    return call(side_by_side, jax.ShapeDtypeStruct((TOK, HEADS * HD), half), [WHOLE])(back)


def solution(mesh):
    grid = Mesh(mesh.devices.reshape(8, 4, 2, 8), ("z", "x", "c", "y"))
    tokens = P(("z", "x", "c", "y"), None)
    return jax.shard_map(
        local, mesh=grid, in_specs=(tokens,) * 3 + (P(),) * 3, out_specs=tokens, check_vma=False
    )
```

profile of v0, /device:TPU:200, one launch (start us, length us, event | category | flops | bytes accessed | tf_op | source)
XLA Modules:
  0.0 112.8 jit_solution(6405769302780006450)
XLA Ops:
  0.0 1.0 copy-done.1
  1.0 1.0 copy-done.2
  2.0 0.7 copy-done.4
  2.7 1.3 %shard_map.64 = bf16[32,2,64,128]{3,2,1,0:T(8,128)(2,1)} custom-call(bf16[64,3072]{1,0:T(8,128)(2,1)S(1)} %copy-done.1, bf16[64,3072]{1,0:T(8,128)(2,1)S(1)} %copy-done.2, f32[1,3072]{1,0:T(1,128)S(1)} %bitcast.19), custom_call_target="tpu_custom_call" | custom-call | bytes 4194304 | tf_op jit(solution)/shard_map/pallas_call | solution.py:281
  4.0 10.3 %all-to-all-start = ((bf16[32,2,64,128]{3,2,1,0:T(8,128)(2,1)}), bf16[32,2,64,128]{3,2,1,0:T(8,128)(2,1)S(1)}, u32[]{:S(2)}, u32[]{:S(2)}) async-start(bf16[32,2,64,128]{3,2,1,0:T(8,128)(2,1)} %shard_map.64), calls=%async_computation | async-start | bytes 2097152 | tf_op jit(solution)/shard_map/all_to_all | solution.py:270
  14.3 0.0 copy-done.3
  14.3 0.0 copy-done.5
  14.3 1.0 shard_map.65
  15.3 27.5 %all-to-all-done = bf16[32,2,64,128]{3,2,1,0:T(8,128)(2,1)S(1)} async-done(((bf16[32,2,64,128]{3,2,1,0:T(8,128)(2,1)}), bf16[32,2,64,128]{3,2,1,0:T(8,128)(2,1)S(1)}, u32[]{:S(2)}, u32[]{:S(2)}) %all-to-all-start) | async-done | bytes 1048608 | tf_op jit(solution)/shard_map/all_to_all | solution.py:270
  42.8 1.9 %collective-permute-start.2 = (bf16[4,2,2,2,2,64,128]{6,5,4,3,2,1,0:T(8,128)(2,1)S(1)}, bf16[4,2,2,2,2,64,128]{6,5,4,3,2,1,0:T(8,128)(2,1)}, u32[]{:S(2)}, u32[]{:S(2)}) collective-permute-start(bf16[4,2,2,2,2,64,128]{6,5,4,3,2,1,0:T(8,128)(2,1)S(1)} %bitcast.11), channel_id=1, source_target_pairs={{64,0},{128,64},{192,128},{256,192},{320,256},{384,320},{448,384},... | collective-permute-start | bytes 3145736 | tf_op jit(solution)/shard_map/ppermute | solution.py:294
  44.7 5.5 %collective-permute-start.1 = (bf16[4,2,2,2,2,64,128]{6,5,4,3,2,1,0:T(8,128)(2,1)S(1)}, bf16[4,2,2,2,2,64,128]{6,5,4,3,2,1,0:T(8,128)(2,1)}, u32[]{:S(2)}, u32[]{:S(2)}) collective-permute-start(bf16[4,2,2,2,2,64,128]{6,5,4,3,2,1,0:T(8,128)(2,1)S(1)} %bitcast.12), channel_id=1, source_target_pairs={{0,64},{64,128},{128,192},{192,256},{256,320},{320,384},{384,448},... | collective-permute-start | bytes 3145736 | tf_op jit(solution)/shard_map/ppermute | solution.py:293
  50.2 1.9 %collective-permute-start = (bf16[4,2,2,2,2,64,128]{6,5,4,3,2,1,0:T(8,128)(2,1)S(1)}, bf16[4,2,2,2,2,64,128]{6,5,4,3,2,1,0:T(8,128)(2,1)S(1)}, u32[]{:S(2)}, u32[]{:S(2)}) collective-permute-start(bf16[4,2,2,2,2,64,128]{6,5,4,3,2,1,0:T(8,128)(2,1)S(1)} %bitcast.13), channel_id=1, source_target_pairs={{0,8},{8,0},{1,9},{9,1},{2,10},{10,2},{3,11},{11,3},{4,12},{12,4},... | collective-permute-start | bytes 3145736 | tf_op jit(solution)/shard_map/ppermute | solution.py:295
  52.1 5.2 %all-to-all-start.1 = ((bf16[32,64,128]{2,1,0:T(8,128)(2,1)}), bf16[32,64,128]{2,1,0:T(8,128)(2,1)S(1)}, u32[]{:S(2)}, u32[]{:S(2)}) async-start(bf16[32,64,128]{2,1,0:T(8,128)(2,1)} %shard_map.65), calls=%async_computation.1 | async-start | bytes 1048576 | tf_op jit(solution)/shard_map/all_to_all | solution.py:270
  57.4 0.0 copy-start.6
  57.4 0.7 copy-done.6
  58.0 0.2 reshape.21
  58.2 0.1 constant_dynamic-slice_fusion
  58.3 0.1 copy.8
  58.4 0.1 reshape.22
  58.5 0.1 pad_add_fusion.meta_ref
  58.6 10.8 %collective-permute-done.2.high_ref = bf16[4,2,2,2,2,64,128]{6,5,4,3,2,1,0:T(8,128)(2,1)} collective-permute-done((bf16[4,2,2,2,2,64,128]{6,5,4,3,2,1,0:T(8,128)(2,1)S(1)}, bf16[4,2,2,2,2,64,128]{6,5,4,3,2,1,0:T(8,128)(2,1)}, u32[]{:S(2)}, u32[]{:S(2)}) %collective-permute-start.2) | collective-permute-done | bytes 1048608 | tf_op jit(solution)/shard_map/ppermute | solution.py:294
  69.4 1.9 %collective-permute-start.4 = (bf16[4,2,2,2,2,64,128]{6,5,4,3,2,1,0:T(8,128)(2,1)}, bf16[4,2,2,2,2,64,128]{6,5,4,3,2,1,0:T(8,128)(2,1)}, u32[]{:S(2)}, u32[]{:S(2)}) collective-permute-start(bf16[4,2,2,2,2,64,128]{6,5,4,3,2,1,0:T(8,128)(2,1)} %collective-permute-done.2.high_ref), channel_id=1, source_target_pairs={{0,8},{8,0},{1,9},{9,1},{2,10},{10,2},{3,11},{11,3},{4,12},{12,4},... | collective-permute-start | bytes 3145736 | tf_op jit(solution)/shard_map/ppermute | solution.py:297
  71.3 0.0 collective-permute-done.1.low
  71.3 2.4 %collective-permute-start.3 = (bf16[4,2,2,2,2,64,128]{6,5,4,3,2,1,0:T(8,128)(2,1)}, bf16[4,2,2,2,2,64,128]{6,5,4,3,2,1,0:T(8,128)(2,1)}, u32[]{:S(2)}, u32[]{:S(2)}) collective-permute-start(bf16[4,2,2,2,2,64,128]{6,5,4,3,2,1,0:T(8,128)(2,1)} %collective-permute-done.1.low), channel_id=1, source_target_pairs={{0,8},{8,0},{1,9},{9,1},{2,10},{10,2},{3,11},{11,3},{4,12},{12,4},... | collective-permute-start | bytes 3145736 | tf_op jit(solution)/shard_map/ppermute | solution.py:296
  73.7 2.0 %all-to-all-done.1 = bf16[32,64,128]{2,1,0:T(8,128)(2,1)S(1)} async-done(((bf16[32,64,128]{2,1,0:T(8,128)(2,1)}), bf16[32,64,128]{2,1,0:T(8,128)(2,1)S(1)}, u32[]{:S(2)}, u32[]{:S(2)}) %all-to-all-start.1) | async-done | bytes 524320 | tf_op jit(solution)/shard_map/all_to_all | solution.py:270
  75.7 0.0 collective-permute-done.theirs_ref.their_own
  75.7 6.4 %shard_map.66 = (f32[8,256,128]{2,1,0:T(8,128)S(1)}, f32[8,256,128]{2,1,0:T(8,128)S(1)}, f32[8,256,128]{2,1,0:T(8,128)S(1)}) custom-call(s32[26]{0:T(128)S(1)} %pad_add_fusion.meta_ref, bf16[4,2,2,2,64,128]{5,4,3,2,1,0:T(8,128)(2,1)S(1)} %bitcast.16, bf16[4,2,2,2,2,64,128]{6,5,4,3,2,1,0:T(8,128)(2,1)S(1)} %bitcast.14, ...), custom_call_target="tpu_custom_call" | custom-call | flops 22817013760 | bytes 4194304 | tf_op jit(solution)/shard_map/pallas_call | solution.py:301
  82.1 0.0 collective-permute-done.4.their_high
  82.1 0.0 collective-permute-done.3.their_low
  82.1 7.3 %shard_map.67 = bf16[4,2,2,2,64,128]{5,4,3,2,1,0:T(8,128)(2,1)S(1)} custom-call(s32[26]{0:T(128)S(1)} %pad_add_fusion.meta_ref, bf16[4,2,2,2,64,128]{5,4,3,2,1,0:T(8,128)(2,1)S(1)} %bitcast.17, f32[8,256,128]{2,1,0:T(8,128)S(1)} %get-tuple-element.16.top_ref, f32[8,256,128]{2,1,0:T(8,128)S(1)} %get-tuple-element.17.lanes_ref, ...), custom_call_target="tpu_custom_call" | custom-call | flops 1476395008 | bytes 4194304 | tf_op jit(solution)/shard_map/pallas_call | solution.py:303
  89.4 22.5 %all_to_all.15.x_ref = bf16[32,64,128]{2,1,0:T(8,128)(2,1)S(1)} all-to-all(bf16[32,64,128]{2,1,0:T(8,128)(2,1)S(1)} %bitcast.18), channel_id=1, replica_groups=mesh['z'=8,'x'=4,'c'=2,'y'=8] {'x','y'}, dimensions={0} | all-to-all | bytes 1048576 | tf_op jit(solution)/shard_map/all_to_all | solution.py:270
  112.0 0.8 shard_map.68
  (7 shorter events, 0.0 us)
Async XLA Ops:
  0.0 1.0 copy-start.1
  1.0 1.0 copy-start.2
  2.0 0.7 copy-start.4
  4.0 10.3 %copy-start.3 = (bf16[64,3072]{1,0:T(8,128)(2,1)S(1)}, bf16[64,3072]{1,0:T(8,128)(2,1)}, u32[]{:S(2)}) copy-start(bf16[64,3072]{1,0:T(8,128)(2,1)} %q_ref) | copy-start | bytes 1179652
  4.0 10.3 %copy-start.5 = (f32[3072]{0:T(1024)S(1)}, f32[3072]{0:T(1024)}, u32[]{:S(2)}) copy-start(f32[3072]{0:T(1024)} %param.9) | copy-start | bytes 36868
  4.0 38.8 %all-to-all-start = ((bf16[32,2,64,128]{3,2,1,0:T(8,128)(2,1)}), bf16[32,2,64,128]{3,2,1,0:T(8,128)(2,1)S(1)}, u32[]{:S(2)}, u32[]{:S(2)}) async-start(bf16[32,2,64,128]{3,2,1,0:T(8,128)(2,1)} %shard_map.64), calls=%async_computation | async-start | bytes 2097152 | tf_op jit(solution)/shard_map/all_to_all | solution.py:270
  42.8 26.6 %collective-permute-start.2 = (bf16[4,2,2,2,2,64,128]{6,5,4,3,2,1,0:T(8,128)(2,1)S(1)}, bf16[4,2,2,2,2,64,128]{6,5,4,3,2,1,0:T(8,128)(2,1)}, u32[]{:S(2)}, u32[]{:S(2)}) collective-permute-start(bf16[4,2,2,2,2,64,128]{6,5,4,3,2,1,0:T(8,128)(2,1)S(1)} %bitcast.11), channel_id=1, source_target_pairs={{64,0},{128,64},{192,128},{256,192},{320,256},{384,320},{448,384},... | collective-permute-start | bytes 3145736 | tf_op jit(solution)/shard_map/ppermute | solution.py:294
  44.7 26.6 %collective-permute-start.1 = (bf16[4,2,2,2,2,64,128]{6,5,4,3,2,1,0:T(8,128)(2,1)S(1)}, bf16[4,2,2,2,2,64,128]{6,5,4,3,2,1,0:T(8,128)(2,1)}, u32[]{:S(2)}, u32[]{:S(2)}) collective-permute-start(bf16[4,2,2,2,2,64,128]{6,5,4,3,2,1,0:T(8,128)(2,1)S(1)} %bitcast.12), channel_id=1, source_target_pairs={{0,64},{64,128},{128,192},{192,256},{256,320},{320,384},{384,448},... | collective-permute-start | bytes 3145736 | tf_op jit(solution)/shard_map/ppermute | solution.py:293
  50.2 25.4 %collective-permute-start = (bf16[4,2,2,2,2,64,128]{6,5,4,3,2,1,0:T(8,128)(2,1)S(1)}, bf16[4,2,2,2,2,64,128]{6,5,4,3,2,1,0:T(8,128)(2,1)S(1)}, u32[]{:S(2)}, u32[]{:S(2)}) collective-permute-start(bf16[4,2,2,2,2,64,128]{6,5,4,3,2,1,0:T(8,128)(2,1)S(1)} %bitcast.13), channel_id=1, source_target_pairs={{0,8},{8,0},{1,9},{9,1},{2,10},{10,2},{3,11},{11,3},{4,12},{12,4},... | collective-permute-start | bytes 3145736 | tf_op jit(solution)/shard_map/ppermute | solution.py:295
  52.1 23.5 %all-to-all-start.1 = ((bf16[32,64,128]{2,1,0:T(8,128)(2,1)}), bf16[32,64,128]{2,1,0:T(8,128)(2,1)S(1)}, u32[]{:S(2)}, u32[]{:S(2)}) async-start(bf16[32,64,128]{2,1,0:T(8,128)(2,1)} %shard_map.65), calls=%async_computation.1 | async-start | bytes 1048576 | tf_op jit(solution)/shard_map/all_to_all | solution.py:270
  57.4 0.7 copy-start.6
  69.4 12.8 %collective-permute-start.4 = (bf16[4,2,2,2,2,64,128]{6,5,4,3,2,1,0:T(8,128)(2,1)}, bf16[4,2,2,2,2,64,128]{6,5,4,3,2,1,0:T(8,128)(2,1)}, u32[]{:S(2)}, u32[]{:S(2)}) collective-permute-start(bf16[4,2,2,2,2,64,128]{6,5,4,3,2,1,0:T(8,128)(2,1)} %collective-permute-done.2.high_ref), channel_id=1, source_target_pairs={{0,8},{8,0},{1,9},{9,1},{2,10},{10,2},{3,11},{11,3},{4,12},{12,4},... | collective-permute-start | bytes 3145736 | tf_op jit(solution)/shard_map/ppermute | solution.py:297
  71.3 10.8 %collective-permute-start.3 = (bf16[4,2,2,2,2,64,128]{6,5,4,3,2,1,0:T(8,128)(2,1)}, bf16[4,2,2,2,2,64,128]{6,5,4,3,2,1,0:T(8,128)(2,1)}, u32[]{:S(2)}, u32[]{:S(2)}) collective-permute-start(bf16[4,2,2,2,2,64,128]{6,5,4,3,2,1,0:T(8,128)(2,1)} %collective-permute-done.1.low), channel_id=1, source_target_pairs={{0,8},{8,0},{1,9},{9,1},{2,10},{10,2},{3,11},{11,3},{4,12},{12,4},... | collective-permute-start | bytes 3145736 | tf_op jit(solution)/shard_map/ppermute | solution.py:296
  75.7 6.4 %copy-start = (bf16[4,2,2,2,2,64,128]{6,5,4,3,2,1,0:T(8,128)(2,1)}, bf16[4,2,2,2,2,64,128]{6,5,4,3,2,1,0:T(8,128)(2,1)S(1)}, u32[]{:S(2)}) copy-start(bf16[4,2,2,2,2,64,128]{6,5,4,3,2,1,0:T(8,128)(2,1)S(1)} %collective-permute-done.theirs_ref.their_own) | copy-start | bytes 3145732
where the time goes:
time: 113 us
  waiting for transfers between devices  40.2 us (36%)
  starting transfers between devices  29.1 us (26%)
  blocking collectives  22.5 us (20%)
  Pallas kernels  16.8 us (15%)
  local copies, waits for them, and re-layouts  3.82 us (3%)
    all_to_all x2, waiting for transfers between devices, exchange(): lax.all_to_all(x, ('x', 'y'), split_axis=0, concat_axis=0, tiled=True)  29.4 us
    all_to_all x1, blocking collectives, exchange(): lax.all_to_all(x, ('x', 'y'), split_axis=0, concat_axis=0, tiled=True)  22.5 us
    all_to_all x2, starting transfers between devices, exchange(): lax.all_to_all(x, ('x', 'y'), split_axis=0, concat_axis=0, tiled=True)  15.5 us
    ppermute x1, waiting for transfers between devices, local(): high = lax.ppermute(mine, 'z', [(n + 1, n) for n in range(7)])  10.8 us
    pallas_call x1, Pallas kernels, local(): call(attend_rest, jax.ShapeDtypeStruct(blocks, half), [TABLE] + [WHOLE] *...  7.28 us
    pallas_call x1, Pallas kernels, local(): call(attend_own, state, [TABLE] + [WHOLE] * 3, flops=OWN_FLOPS, scratch=s...  6.44 us
    ppermute x1, starting transfers between devices, local(): low = lax.ppermute(mine, 'z', [(n, n + 1) for n in range(7)])  5.49 us
    unnamed x14, local copies, waits for them, and re-layouts  3.39 us
  transfers between devices with their start and end apart: 7, of which 3 were waited for; matrix products, arithmetic and copies ran while one was open for 0% of the time, Pallas kernels for 7%

commit v1 on v0

v1 whole, which is shorter than its diff:
```python
import math

import jax
import jax.numpy as jnp
from jax import lax
from jax.experimental import pallas as pl
from jax.experimental.pallas import tpu as pltpu
from jax.sharding import Mesh
from jax.sharding import PartitionSpec as P

HD = 128
HEADS = 24
TOK = 64
SLOTS = 32
LOG2E = 1.4426950408889634
FACTOR = LOG2E / math.sqrt(HD)
VMEM_LIMIT = 48 * 1024 * 1024
PREPARE_LIMIT = 60 * 1024 * 1024
WHOLE = pl.BlockSpec(memory_space=pltpu.VMEM)
TABLE = pl.BlockSpec(memory_space=pltpu.SMEM)
ANYWHERE = pl.BlockSpec(memory_space=pl.ANY)


DISTANCES = (0, 1, -1, 2, -2, 3, -3, 4, -4, 6, -6, 5, -5, 7, -7)


def normed(x_ref, gain_ref):
    x = x_ref[...].astype(jnp.float32)
    mean_square = jnp.mean(x * x, axis=-1, keepdims=True)
    return (x * lax.rsqrt(mean_square + 1e-06) * gain_ref[...]).astype(jnp.bfloat16)


def spread(x, out_ref):
    for h in range(HEADS):
        out_ref[h] = x[:, h * HD : (h + 1) * HD]
    for h in range(HEADS, SLOTS):
        out_ref[h] = jnp.zeros(out_ref.shape[1:], out_ref.dtype)


def prepare_kv(k_hbm, v_hbm, gain_hbm, out_ref, k_ref, v_ref, gain_ref, sems):
    pairs = ((k_hbm, k_ref), (gain_hbm, gain_ref), (v_hbm, v_ref))
    loads = [pltpu.make_async_copy(src, dst, sems.at[n]) for n, (src, dst) in enumerate(pairs)]
    for load in loads:
        load.start()
    loads[0].wait()
    loads[1].wait()
    spread(normed(k_ref, gain_ref), out_ref.at[:, 0])
    loads[2].wait()
    spread(v_ref, out_ref.at[:, 1])


def prepare_q(q_ref, gain_ref, out_ref):
    spread(normed(q_ref, gain_ref), out_ref)


def lane_fold(op, matrix):
    parts = [matrix[:, n : n + HD] for n in range(0, matrix.shape[1], HD)]
    while len(parts) > 1:
        parts = [op(*parts[n : n + 2]) if n + 1 < len(parts) else parts[n] for n in range(0, len(parts), 2)]
    return parts[0]


def width(d):
    return 512 if abs(d) <= 1 else 256 if abs(d) <= 3 else 128


def place(i, d):
    if d % 2 == 0:
        n = 4 + i + d // 2
        return n, "low" if n < 4 else "high" if n >= 8 else None
    n = 4 + i + (d - 1) // 2
    return n, "low" if n < 3 else "edge_low" if n == 3 else "high" if n >= 8 else "edge_high" if n == 7 else None


class Unit:
    def __init__(self, meta_ref, i, parity, odd, keys, values):
        self.i = i
        self.parity = parity
        self.offs = [[meta_ref[2 + (i * 3 + level) * 2 + side] for side in range(2)] for level in range(3)]
        self.keys = keys
        self.values = values
        used = [d for d in DISTANCES if d % 2 == odd]
        self.both = []
        self.far = []
        for size, groups in ((512, self.both), (256, self.both), (128, self.far)):
            here = [d for d in used if width(d) == size]
            per = 512 // size
            groups += [here[n : n + per] for n in range(0, len(here), per)]

    def q(self, q_ref, high):
        return q_ref[self.i, :, high, self.parity].reshape(HD, HD)

    def gather(self, fetch, group, cls):
        parts = []
        for d in group:
            side = 0 if d < 0 else 1
            if abs(d) <= 1:
                at = (slice(None),) * 3
            elif abs(d) <= 3:
                at = (slice(None), slice(None), (cls + self.offs[1][side]) & 1)
            else:
                kept = (cls + self.offs[2][side]) & 3
                at = (slice(None), kept >> 1, kept & 1)
            parts.append(fetch(self.i, d, at).reshape(width(d), HD))
        return jnp.concatenate(parts, axis=0)


def store_scores(unit, q, group, cls, s_ref, rows, start, bias):
    key = unit.gather(unit.keys, group, cls)
    s = lax.dot_general(q, key, (((1,), (1,)), ((), ())), preferred_element_type=jnp.float32)
    size = width(group[0])
    parts = [s[:, m * size : (m + 1) * size] for m in range(len(group))]
    for m, d in enumerate(group):
        kind = place(unit.i, d)[1]
        parts[m] = parts[m] if kind is None else parts[m] + bias[kind]
    s = jnp.concatenate(parts, axis=1)
    s_ref[rows, start : start + key.shape[0]] = s
    return lane_fold(jnp.maximum, s), start + key.shape[0]


def score(unit, q_ref, s_ref, bias, before=None):
    q = [unit.q(q_ref, high) for high in range(2)]
    both = jnp.concatenate(q, axis=0)
    top = before
    start = 0
    for group in unit.both:
        part, start = store_scores(unit, both, group, unit.parity, s_ref, slice(0, 256), start, bias)
        top = part if top is None else jnp.maximum(top, part)
    tops = []
    for high in range(2):
        rows = slice(high * HD, (high + 1) * HD)
        own = top[rows]
        at = start
        for group in unit.far:
            part, at = store_scores(unit, q[high], group, unit.parity + 2 * high, s_ref, rows, at, bias)
            own = jnp.maximum(own, part)
        tops.append(jnp.max(own, axis=1, keepdims=True))
    return tops


def mix(unit, tops, s_ref):
    shift = jnp.concatenate(tops, axis=0) * FACTOR
    sums = {}

    def weigh(rows, start, group, moved):
        size = width(group[0])
        weights = jnp.exp2(s_ref[rows, start : start + size * len(group)] * FACTOR - moved)
        key = (rows.start, rows.stop)
        for m in range(len(group)):
            part = lane_fold(jnp.add, weights[:, m * size : (m + 1) * size])
            sums[key] = sums[key] + part if key in sums else part
        return weights.astype(jnp.bfloat16)

    total = None
    start = 0
    for group in unit.both:
        w = weigh(slice(0, 256), start, group, shift)
        start += w.shape[1]
        mixed = jnp.dot(w, unit.gather(unit.values, group, unit.parity), preferred_element_type=jnp.float32)
        total = mixed if total is None else total + mixed
    result = []
    for high in range(2):
        rows = slice(high * HD, (high + 1) * HD)
        own = total[rows]
        at = start
        for group in unit.far:
            w = weigh(rows, at, group, shift[rows])
            at += w.shape[1]
            value = unit.gather(unit.values, group, unit.parity + 2 * high)
            own = own + jnp.dot(w, value, preferred_element_type=jnp.float32)
        lanes = None
        for (first, last), part in sums.items():
            if not first <= rows.start < last:
                continue
            if last - first == 256:
                part = part[rows]
            lanes = part if lanes is None else lanes + part
        result.append((lanes, own))
    return result


def biases(meta_ref):
    z = meta_ref[0]
    core = meta_ref[1]
    usable = {
        "low": z > 0,
        "edge_low": (z > 0) | (core == 1),
        "edge_high": (z < 7) | (core == 0),
        "high": z < 7,
    }
    return {kind: jnp.where(inside, 0.0, -1e30).astype(jnp.float32) for kind, inside in usable.items()}


def attend_mine(meta_ref, q_ref, low, own_ref, high_ref, top_ref, lanes_ref, total_ref, s_even, s_odd):
    bias = biases(meta_ref)

    def fetch(which):
        def of(i, d, at):
            n = place(i, d)[0]
            return (low, own_ref, high_ref)[n // 4][(n % 4,) + at + (which,)]

        return of

    units = [Unit(meta_ref, i, parity, 0, fetch(0), fetch(1)) for i in range(4) for parity in range(2)]
    s_refs = (s_even, s_odd)
    tops = score(units[0], q_ref, s_refs[0], bias)
    for n, unit in enumerate(units):
        now = tops
        if n + 1 < len(units):
            tops = score(units[n + 1], q_ref, s_refs[(n + 1) % 2], bias)
        for high, (lanes, own) in enumerate(mix(unit, now, s_refs[n % 2])):
            rows = slice(high * HD, (high + 1) * HD)
            top_ref[n, rows] = jnp.broadcast_to(now[high], (HD, HD))
            lanes_ref[n, rows] = lanes
            total_ref[n, rows] = own


def attend_theirs(
    meta_ref, q_ref, top_ref, lanes_ref, total_ref, low, own_ref, high_ref, out_ref, k_ref, v_ref, s_even, s_odd, sems
):
    first = 1 - meta_ref[1]
    sources = ((low, first), (own_ref, first + 4), (high_ref, first + 8))

    def load(src, which, ref, slot, n):
        made = pltpu.make_async_copy(src.at[:, :, :, :, which], ref.at[pl.ds(slot, 4)], sems.at[n])
        made.start()
        return made

    k_copies = [load(src, 0, k_ref, slot, n) for n, (src, slot) in enumerate(sources)]
    v_copies = [load(src, 1, v_ref, slot, n + 3) for n, (src, slot) in enumerate(sources)]
    bias = biases(meta_ref)

    def keys(i, d, at):
        return k_ref[(place(i, d)[0] + 1,) + at]

    def values(i, d, at):
        return v_ref[(place(i, d)[0] + 1,) + at]

    units = [Unit(meta_ref, i, parity, 1, keys, values) for i in range(4) for parity in range(2)]
    s_refs = (s_even, s_odd)
    for made in k_copies:
        made.wait()
    tops = score(units[0], q_ref, s_refs[0], bias, top_ref[0])
    for made in v_copies:
        made.wait()
    for n, unit in enumerate(units):
        now = tops
        if n + 1 < len(units):
            tops = score(units[n + 1], q_ref, s_refs[(n + 1) % 2], bias, top_ref[n + 1])
        for high, (lanes, mixed) in enumerate(mix(unit, now, s_refs[n % 2])):
            rows = slice(high * HD, (high + 1) * HD)
            carried = jnp.exp2((top_ref[n, rows] - now[high]) * FACTOR)
            lanes = lanes + lanes_ref[n, rows] * carried
            mixed = mixed + total_ref[n, rows] * carried
            row_sum = jnp.sum(lanes, axis=1, keepdims=True)
            out_ref[unit.i, :, high, unit.parity] = (mixed / row_sum).astype(jnp.bfloat16).reshape(2, TOK, HD)


def side_by_side(x_ref, out_ref):
    for h in range(HEADS):
        out_ref[:, h * HD : (h + 1) * HD] = x_ref[h]


def call(kernel, out_shape, specs, flops=0, scratch=(), limit=VMEM_LIMIT, **more):
    params = pltpu.CompilerParams(vmem_limit_bytes=limit)
    cost = pl.CostEstimate(flops=flops, bytes_accessed=4 << 20, transcendentals=flops // 512)
    return pl.pallas_call(
        kernel, out_shape=out_shape, in_specs=specs, scratch_shapes=scratch,
        compiler_params=params, cost_estimate=cost, **more,
    )


def exchange(x):
    return lax.all_to_all(x, ("x", "y"), split_axis=0, concat_axis=0, tiled=True)


def local(queries, keys, values, q_gain, k_gain, block_offset):
    half = jnp.bfloat16
    z = lax.axis_index("z")
    core = lax.axis_index("c")
    frame = lax.dynamic_slice_in_dim(block_offset.reshape(8, 4, 2, 6), z, 1, 0)
    table = lax.dynamic_slice_in_dim(frame, core, 1, 2).reshape(24)
    meta = jnp.concatenate([jnp.stack([z, core]).astype(jnp.int32), table])

    tokens = pltpu.VMEM((TOK, HEADS * HD), half)
    kv = call(
        prepare_kv,
        jax.ShapeDtypeStruct((SLOTS, 2, TOK, HD), half),
        [ANYWHERE] * 3,
        scratch=[tokens, tokens, pltpu.VMEM((1, HEADS * HD), jnp.float32), pltpu.SemaphoreType.DMA((3,))],
        limit=PREPARE_LIMIT,
    )(keys, values, k_gain.reshape(1, -1))
    queries, kv = lax.optimization_barrier((queries, kv))
    q = call(prepare_q, jax.ShapeDtypeStruct((SLOTS, TOK, HD), half), [WHOLE] * 2)(queries, q_gain.reshape(1, -1))
    kv = exchange(kv)
    q, kv = lax.optimization_barrier((q, kv))
    blocks = (4, 2, 2, 2, TOK, HD)
    q = exchange(q).reshape(blocks)

    mine = kv.reshape(4, 2, 2, 2, 2, TOK, HD)
    swap = [(0, 1), (1, 0)]
    low = lax.ppermute(mine, "z", [(n, n + 1) for n in range(7)])
    high = lax.ppermute(mine, "z", [(n + 1, n) for n in range(7)])
    theirs = lax.ppermute(mine, "c", swap)
    their_low = lax.ppermute(low, "c", swap)
    their_high = lax.ppermute(high, "c", swap)

    state = [jax.ShapeDtypeStruct((8, 256, HD), jnp.float32)] * 3
    state = call(
        attend_mine,
        state,
        [TABLE] + [WHOLE] * 4,
        flops=4 * 4 * 1536 * 512 * HD,
        scratch=[pltpu.VMEM((256, 1536), jnp.float32)] * 2,
    )(meta, q, low, mine, high)
    kept = pltpu.VMEM((13, 2, 2, 2, TOK, HD), half)
    out = call(
        attend_theirs,
        jax.ShapeDtypeStruct(blocks, half),
        [TABLE] + [WHOLE] * 4 + [ANYWHERE] * 3,
        flops=4 * 4 * 2048 * 512 * HD,
        scratch=[kept, kept] + [pltpu.VMEM((256, 2048), jnp.float32)] * 2 + [pltpu.SemaphoreType.DMA((6,))],
    )(meta, q, *state, their_low, theirs, their_high)
    back = exchange(out.reshape(SLOTS, TOK, HD))
    return call(side_by_side, jax.ShapeDtypeStruct((TOK, HEADS * HD), half), [WHOLE])(back)


def solution(mesh):
    grid = Mesh(mesh.devices.reshape(8, 4, 2, 8), ("z", "x", "c", "y"))
    tokens = P(("z", "x", "c", "y"), None)
    return jax.shard_map(
        local, mesh=grid, in_specs=(tokens,) * 3 + (P(),) * 3, out_specs=tokens, check_vma=False
    )
```

time: 113 us -> 115 us (1.018)
  local copies, waits for them, and re-layouts: 3.82 us -> 1.13 us
  blocking collectives: 22.5 us -> 25 us
  waiting for transfers between devices: 40.2 us -> 42.2 us
    ppermute x1, waiting for transfers between devices: 0.01 us -> 11.2 us  [local(): low = lax.ppermute(mine, 'z', [(n, n + 1) for n in range(7)])]
    ppermute x1, waiting for transfers between devices: 10.8 us -> 3.52 us  [local(): high = lax.ppermute(mine, 'z', [(n + 1, n) for n in range(7)])]
    unnamed x14 -> x6, local copies, waits for them, and re-layouts: 3.39 us -> 0.69 us
    all_to_all x1, blocking collectives: 22.5 us -> 25 us  [exchange(): lax.all_to_all(x, ('x', 'y'), split_axis=0, concat_axis=0, tiled=True)]
    all_to_all x2, waiting for transfers between devices: 29.4 us -> 27.5 us  [exchange(): lax.all_to_all(x, ('x', 'y'), split_axis=0, concat_axis=0, tiled=True)]
  transfers between devices with their start and end apart: 7 -> 7, of which waited for: 3 -> 3; matrix products, arithmetic and copies ran while one was open for 0% -> 0% of each run, Pallas kernels for 7% -> 6%
where the time goes in v1:
time: 115 us
  waiting for transfers between devices  42.2 us (37%)
  starting transfers between devices  28.6 us (25%)
  blocking collectives  25 us (22%)
  Pallas kernels  17.7 us (15%)
    all_to_all x2, waiting for transfers between devices, exchange(): lax.all_to_all(x, ('x', 'y'), split_axis=0, concat_axis=0, tiled=True)  27.5 us
    all_to_all x1, blocking collectives, exchange(): lax.all_to_all(x, ('x', 'y'), split_axis=0, concat_axis=0, tiled=True)  25 us
    all_to_all x2, starting transfers between devices, exchange(): lax.all_to_all(x, ('x', 'y'), split_axis=0, concat_axis=0, tiled=True)  15.5 us
    ppermute x1, waiting for transfers between devices, local(): low = lax.ppermute(mine, 'z', [(n, n + 1) for n in range(7)])  11.2 us
    pallas_call x1, Pallas kernels, local(): call(attend_theirs, jax.ShapeDtypeStruct(blocks, half), [TABLE] + [WHOLE]...  8.11 us
    ppermute x1, starting transfers between devices, local(): low = lax.ppermute(mine, 'z', [(n, n + 1) for n in range(7)])  5.48 us
    pallas_call x1, Pallas kernels, local(): call(attend_mine, state, [TABLE] + [WHOLE] * 4, flops=4 * 4 * 1536 * 512...  5.47 us
    ppermute x1, waiting for transfers between devices, local(): high = lax.ppermute(mine, 'z', [(n + 1, n) for n in range(7)])  3.52 us
  transfers between devices with their start and end apart: 7, of which 3 were waited for; matrix products, arithmetic and copies ran while one was open for 0% of the time, Pallas kernels for 6%

profile of v1, /device:TPU:200, one launch (start us, length us, event | category | flops | bytes accessed | tf_op | source)
XLA Modules:
  0.0 114.9 jit_solution(7749271837624670191)
XLA Ops:
  0.0 2.3 %shard_map.64 = bf16[32,2,64,128]{3,2,1,0:T(8,128)(2,1)} custom-call(bf16[64,3072]{1,0:T(8,128)(2,1)} %k_hbm.1, bf16[64,3072]{1,0:T(8,128)(2,1)} %v_hbm.1, f32[1,3072]{1,0:T(1,128)} %bitcast.19), custom_call_target="tpu_custom_call" | custom-call | bytes 4194304 | tf_op jit(solution)/shard_map/pallas_call | solution.py:286
  2.3 0.0 copy-start
  2.3 0.0 copy-start.1
  2.3 10.3 %all-to-all-start = ((bf16[32,2,64,128]{3,2,1,0:T(8,128)(2,1)}), bf16[32,2,64,128]{3,2,1,0:T(8,128)(2,1)S(1)}, u32[]{:S(2)}, u32[]{:S(2)}) async-start(bf16[32,2,64,128]{3,2,1,0:T(8,128)(2,1)} %shard_map.64), calls=%async_computation | async-start | bytes 2097152 | tf_op jit(solution)/shard_map/all_to_all | solution.py:274
  12.6 0.0 copy-done
  12.6 0.0 copy-done.1
  12.7 1.0 shard_map.65
  13.7 27.5 %all-to-all-done = bf16[32,2,64,128]{3,2,1,0:T(8,128)(2,1)S(1)} async-done(((bf16[32,2,64,128]{3,2,1,0:T(8,128)(2,1)}), bf16[32,2,64,128]{3,2,1,0:T(8,128)(2,1)S(1)}, u32[]{:S(2)}, u32[]{:S(2)}) %all-to-all-start) | async-done | bytes 1048608 | tf_op jit(solution)/shard_map/all_to_all | solution.py:274
  41.2 5.5 %collective-permute-start = (bf16[4,2,2,2,2,64,128]{6,5,4,3,2,1,0:T(8,128)(2,1)S(1)}, bf16[4,2,2,2,2,64,128]{6,5,4,3,2,1,0:T(8,128)(2,1)S(1)}, u32[]{:S(2)}, u32[]{:S(2)}) collective-permute-start(bf16[4,2,2,2,2,64,128]{6,5,4,3,2,1,0:T(8,128)(2,1)S(1)} %bitcast.11), channel_id=1, source_target_pairs={{0,64},{64,128},{128,192},{192,256},{256,320},{320,384},{384,448},... | collective-permute-start | bytes 3145736 | tf_op jit(solution)/shard_map/ppermute | solution.py:302
  46.7 1.9 %collective-permute-start.1 = (bf16[4,2,2,2,2,64,128]{6,5,4,3,2,1,0:T(8,128)(2,1)S(1)}, bf16[4,2,2,2,2,64,128]{6,5,4,3,2,1,0:T(8,128)(2,1)}, u32[]{:S(2)}, u32[]{:S(2)}) collective-permute-start(bf16[4,2,2,2,2,64,128]{6,5,4,3,2,1,0:T(8,128)(2,1)S(1)} %bitcast.12), channel_id=1, source_target_pairs={{64,0},{128,64},{192,128},{256,192},{320,256},{384,320},{448,384},... | collective-permute-start | bytes 3145736 | tf_op jit(solution)/shard_map/ppermute | solution.py:303
  48.6 5.2 %all-to-all-start.1 = ((bf16[32,64,128]{2,1,0:T(8,128)(2,1)}), bf16[32,64,128]{2,1,0:T(8,128)(2,1)S(1)}, u32[]{:S(2)}, u32[]{:S(2)}) async-start(bf16[32,64,128]{2,1,0:T(8,128)(2,1)} %shard_map.65), calls=%async_computation.1 | async-start | bytes 1048576 | tf_op jit(solution)/shard_map/all_to_all | solution.py:274
  53.8 1.9 %collective-permute-start.3 = (bf16[4,2,2,2,2,64,128]{6,5,4,3,2,1,0:T(8,128)(2,1)S(1)}, bf16[4,2,2,2,2,64,128]{6,5,4,3,2,1,0:T(8,128)(2,1)}, u32[]{:S(2)}, u32[]{:S(2)}) collective-permute-start(bf16[4,2,2,2,2,64,128]{6,5,4,3,2,1,0:T(8,128)(2,1)S(1)} %bitcast.13), channel_id=1, source_target_pairs={{0,8},{8,0},{1,9},{9,1},{2,10},{10,2},{3,11},{11,3},{4,12},{12,4},... | collective-permute-start | bytes 3145736 | tf_op jit(solution)/shard_map/ppermute | solution.py:304
  55.7 11.2 %collective-permute-done.low = bf16[4,2,2,2,2,64,128]{6,5,4,3,2,1,0:T(8,128)(2,1)S(1)} collective-permute-done((bf16[4,2,2,2,2,64,128]{6,5,4,3,2,1,0:T(8,128)(2,1)S(1)}, bf16[4,2,2,2,2,64,128]{6,5,4,3,2,1,0:T(8,128)(2,1)S(1)}, u32[]{:S(2)}, u32[]{:S(2)}) %collective-permute-start) | collective-permute-done | bytes 1048608 | tf_op jit(solution)/shard_map/ppermute | solution.py:302
  66.9 1.9 %collective-permute-start.2 = (bf16[4,2,2,2,2,64,128]{6,5,4,3,2,1,0:T(8,128)(2,1)S(1)}, bf16[4,2,2,2,2,64,128]{6,5,4,3,2,1,0:T(8,128)(2,1)}, u32[]{:S(2)}, u32[]{:S(2)}) collective-permute-start(bf16[4,2,2,2,2,64,128]{6,5,4,3,2,1,0:T(8,128)(2,1)S(1)} %collective-permute-done.low), channel_id=1, source_target_pairs={{0,8},{8,0},{1,9},{9,1},{2,10},{10,2},{3,11},{11,3},{4,12},{12,4},... | collective-permute-start | bytes 3145736 | tf_op jit(solution)/shard_map/ppermute | solution.py:305
  68.8 3.5 %collective-permute-done.1.high_ref = bf16[4,2,2,2,2,64,128]{6,5,4,3,2,1,0:T(8,128)(2,1)} collective-permute-done((bf16[4,2,2,2,2,64,128]{6,5,4,3,2,1,0:T(8,128)(2,1)S(1)}, bf16[4,2,2,2,2,64,128]{6,5,4,3,2,1,0:T(8,128)(2,1)}, u32[]{:S(2)}, u32[]{:S(2)}) %collective-permute-start.1) | collective-permute-done | bytes 1048608 | tf_op jit(solution)/shard_map/ppermute | solution.py:303
  72.3 1.9 %collective-permute-start.4 = (bf16[4,2,2,2,2,64,128]{6,5,4,3,2,1,0:T(8,128)(2,1)}, bf16[4,2,2,2,2,64,128]{6,5,4,3,2,1,0:T(8,128)(2,1)}, u32[]{:S(2)}, u32[]{:S(2)}) collective-permute-start(bf16[4,2,2,2,2,64,128]{6,5,4,3,2,1,0:T(8,128)(2,1)} %collective-permute-done.1.high_ref), channel_id=1, source_target_pairs={{0,8},{8,0},{1,9},{9,1},{2,10},{10,2},{3,11},{11,3},{4,12},{12,4},... | collective-permute-start | bytes 3145736 | tf_op jit(solution)/shard_map/ppermute | solution.py:306
  74.2 0.0 copy-start.2
  74.2 0.7 copy-done.2
  74.9 0.2 reshape.21
  75.1 0.1 constant_dynamic-slice_fusion
  75.2 0.1 copy.8
  75.3 0.1 reshape.22
  75.4 0.1 pad_add_fusion.meta_ref
  75.5 0.0 all-to-all-done.1
  75.5 5.5 %shard_map.66 = (f32[8,256,128]{2,1,0:T(8,128)S(1)}, f32[8,256,128]{2,1,0:T(8,128)S(1)}, f32[8,256,128]{2,1,0:T(8,128)S(1)}) custom-call(s32[26]{0:T(128)S(1)} %pad_add_fusion.meta_ref, bf16[4,2,2,2,64,128]{5,4,3,2,1,0:T(8,128)(2,1)S(1)} %bitcast.15, bf16[4,2,2,2,2,64,128]{6,5,4,3,2,1,0:T(8,128)(2,1)S(1)} %collective-permute-done.low, ...), custom_call_target="tpu_custom_call" | custom-call | flops 1610612736 | bytes 4194304 | tf_op jit(solution)/shard_map/pallas_call | solution.py:309
  80.9 0.0 collective-permute-done.3.own_ref
  81.0 0.0 collective-permute-done.2.low
  81.0 0.0 collective-permute-done.4.high_ref
  81.0 8.1 %shard_map.67 = bf16[4,2,2,2,64,128]{5,4,3,2,1,0:T(8,128)(2,1)S(1)} custom-call(s32[26]{0:T(128)S(1)} %pad_add_fusion.meta_ref, bf16[4,2,2,2,64,128]{5,4,3,2,1,0:T(8,128)(2,1)S(1)} %bitcast.16, f32[8,256,128]{2,1,0:T(8,128)S(1)} %get-tuple-element.16.top_ref, f32[8,256,128]{2,1,0:T(8,128)S(1)} %get-tuple-element.17.lanes_ref, ...), custom_call_target="tpu_custom_call" | custom-call | flops 2147483648 | bytes 4194304 | tf_op jit(solution)/shard_map/pallas_call | solution.py:317
  89.1 25.0 %all_to_all.15.x_ref = bf16[32,64,128]{2,1,0:T(8,128)(2,1)S(1)} all-to-all(bf16[32,64,128]{2,1,0:T(8,128)(2,1)S(1)} %bitcast.17), channel_id=1, replica_groups=mesh['z'=8,'x'=4,'c'=2,'y'=8] {'x','y'}, dimensions={0} | all-to-all | bytes 1048576 | tf_op jit(solution)/shard_map/all_to_all | solution.py:274
  114.1 0.8 shard_map.68
Async XLA Ops:
  2.3 10.3 %copy-start = (bf16[64,3072]{1,0:T(8,128)(2,1)S(1)}, bf16[64,3072]{1,0:T(8,128)(2,1)}, u32[]{:S(2)}) copy-start(bf16[64,3072]{1,0:T(8,128)(2,1)} %q_ref) | copy-start | bytes 1179652
  2.3 10.3 %copy-start.1 = (f32[3072]{0:T(1024)S(1)}, f32[3072]{0:T(1024)}, u32[]{:S(2)}) copy-start(f32[3072]{0:T(1024)} %param.9) | copy-start | bytes 36868
  2.3 38.8 %all-to-all-start = ((bf16[32,2,64,128]{3,2,1,0:T(8,128)(2,1)}), bf16[32,2,64,128]{3,2,1,0:T(8,128)(2,1)S(1)}, u32[]{:S(2)}, u32[]{:S(2)}) async-start(bf16[32,2,64,128]{3,2,1,0:T(8,128)(2,1)} %shard_map.64), calls=%async_computation | async-start | bytes 2097152 | tf_op jit(solution)/shard_map/all_to_all | solution.py:274
  41.2 25.7 %collective-permute-start = (bf16[4,2,2,2,2,64,128]{6,5,4,3,2,1,0:T(8,128)(2,1)S(1)}, bf16[4,2,2,2,2,64,128]{6,5,4,3,2,1,0:T(8,128)(2,1)S(1)}, u32[]{:S(2)}, u32[]{:S(2)}) collective-permute-start(bf16[4,2,2,2,2,64,128]{6,5,4,3,2,1,0:T(8,128)(2,1)S(1)} %bitcast.11), channel_id=1, source_target_pairs={{0,64},{64,128},{128,192},{192,256},{256,320},{320,384},{384,448},... | collective-permute-start | bytes 3145736 | tf_op jit(solution)/shard_map/ppermute | solution.py:302
  46.7 25.7 %collective-permute-start.1 = (bf16[4,2,2,2,2,64,128]{6,5,4,3,2,1,0:T(8,128)(2,1)S(1)}, bf16[4,2,2,2,2,64,128]{6,5,4,3,2,1,0:T(8,128)(2,1)}, u32[]{:S(2)}, u32[]{:S(2)}) collective-permute-start(bf16[4,2,2,2,2,64,128]{6,5,4,3,2,1,0:T(8,128)(2,1)S(1)} %bitcast.12), channel_id=1, source_target_pairs={{64,0},{128,64},{192,128},{256,192},{320,256},{384,320},{448,384},... | collective-permute-start | bytes 3145736 | tf_op jit(solution)/shard_map/ppermute | solution.py:303
  48.6 26.9 %all-to-all-start.1 = ((bf16[32,64,128]{2,1,0:T(8,128)(2,1)}), bf16[32,64,128]{2,1,0:T(8,128)(2,1)S(1)}, u32[]{:S(2)}, u32[]{:S(2)}) async-start(bf16[32,64,128]{2,1,0:T(8,128)(2,1)} %shard_map.65), calls=%async_computation.1 | async-start | bytes 1048576 | tf_op jit(solution)/shard_map/all_to_all | solution.py:274
  53.8 27.2 %collective-permute-start.3 = (bf16[4,2,2,2,2,64,128]{6,5,4,3,2,1,0:T(8,128)(2,1)S(1)}, bf16[4,2,2,2,2,64,128]{6,5,4,3,2,1,0:T(8,128)(2,1)}, u32[]{:S(2)}, u32[]{:S(2)}) collective-permute-start(bf16[4,2,2,2,2,64,128]{6,5,4,3,2,1,0:T(8,128)(2,1)S(1)} %bitcast.13), channel_id=1, source_target_pairs={{0,8},{8,0},{1,9},{9,1},{2,10},{10,2},{3,11},{11,3},{4,12},{12,4},... | collective-permute-start | bytes 3145736 | tf_op jit(solution)/shard_map/ppermute | solution.py:304
  66.9 14.1 %collective-permute-start.2 = (bf16[4,2,2,2,2,64,128]{6,5,4,3,2,1,0:T(8,128)(2,1)S(1)}, bf16[4,2,2,2,2,64,128]{6,5,4,3,2,1,0:T(8,128)(2,1)}, u32[]{:S(2)}, u32[]{:S(2)}) collective-permute-start(bf16[4,2,2,2,2,64,128]{6,5,4,3,2,1,0:T(8,128)(2,1)S(1)} %collective-permute-done.low), channel_id=1, source_target_pairs={{0,8},{8,0},{1,9},{9,1},{2,10},{10,2},{3,11},{11,3},{4,12},{12,4},... | collective-permute-start | bytes 3145736 | tf_op jit(solution)/shard_map/ppermute | solution.py:305
  72.3 8.7 %collective-permute-start.4 = (bf16[4,2,2,2,2,64,128]{6,5,4,3,2,1,0:T(8,128)(2,1)}, bf16[4,2,2,2,2,64,128]{6,5,4,3,2,1,0:T(8,128)(2,1)}, u32[]{:S(2)}, u32[]{:S(2)}) collective-permute-start(bf16[4,2,2,2,2,64,128]{6,5,4,3,2,1,0:T(8,128)(2,1)} %collective-permute-done.1.high_ref), channel_id=1, source_target_pairs={{0,8},{8,0},{1,9},{9,1},{2,10},{10,2},{3,11},{11,3},{4,12},{12,4},... | collective-permute-start | bytes 3145736 | tf_op jit(solution)/shard_map/ppermute | solution.py:306
  74.2 0.7 copy-start.2

commit v2 on v1

--- a/solution.py
+++ b/solution.py
@@ -1,3 +1,4 @@
+import itertools
 import math
 
 import jax
@@ -21,6 +22,7 @@
 ANYWHERE = pl.BlockSpec(memory_space=pl.ANY)
 
 
+META = 26
 DISTANCES = (0, 1, -1, 2, -2, 3, -3, 4, -4, 6, -6, 5, -5, 7, -7)
 
 
@@ -49,8 +51,10 @@
     spread(v_ref, out_ref.at[:, 1])
 
 
-def prepare_q(q_ref, gain_ref, out_ref):
+def prepare_q(q_ref, gain_ref, meta_ref, out_ref, meta_out):
     spread(normed(q_ref, gain_ref), out_ref)
+    for n in range(META):
+        meta_out[n] = meta_ref[n]
 
 
 def lane_fold(op, matrix):
@@ -118,7 +122,7 @@
     return lane_fold(jnp.maximum, s), start + key.shape[0]
 
 
-def score(unit, q_ref, s_ref, bias, before=None):
+def score(unit, q_ref, s_ref, bias, before, tops):
     q = [unit.q(q_ref, high) for high in range(2)]
     both = jnp.concatenate(q, axis=0)
     top = before
@@ -126,7 +130,7 @@
     for group in unit.both:
         part, start = store_scores(unit, both, group, unit.parity, s_ref, slice(0, 256), start, bias)
         top = part if top is None else jnp.maximum(top, part)
-    tops = []
+        yield
     for high in range(2):
         rows = slice(high * HD, (high + 1) * HD)
         own = top[rows]
@@ -134,49 +138,41 @@
         for group in unit.far:
             part, at = store_scores(unit, q[high], group, unit.parity + 2 * high, s_ref, rows, at, bias)
             own = jnp.maximum(own, part)
+            yield
         tops.append(jnp.max(own, axis=1, keepdims=True))
-    return tops
-
-
-def mix(unit, tops, s_ref):
+
+
+def mix(unit, tops, s_ref, result):
     shift = jnp.concatenate(tops, axis=0) * FACTOR
-    sums = {}
 
     def weigh(rows, start, group, moved):
         size = width(group[0])
         weights = jnp.exp2(s_ref[rows, start : start + size * len(group)] * FACTOR - moved)
-        key = (rows.start, rows.stop)
-        for m in range(len(group)):
-            part = lane_fold(jnp.add, weights[:, m * size : (m + 1) * size])
-            sums[key] = sums[key] + part if key in sums else part
-        return weights.astype(jnp.bfloat16)
+        return weights.astype(jnp.bfloat16), lane_fold(jnp.add, weights)
 
     total = None
+    sums = None
     start = 0
     for group in unit.both:
-        w = weigh(slice(0, 256), start, group, shift)
+        w, part = weigh(slice(0, 256), start, group, shift)
         start += w.shape[1]
         mixed = jnp.dot(w, unit.gather(unit.values, group, unit.parity), preferred_element_type=jnp.float32)
         total = mixed if total is None else total + mixed
-    result = []
+        sums = part if sums is None else sums + part
+        yield
     for high in range(2):
         rows = slice(high * HD, (high + 1) * HD)
         own = total[rows]
+        lanes = sums[rows]
         at = start
         for group in unit.far:
-            w = weigh(rows, at, group, shift[rows])
+            w, part = weigh(rows, at, group, shift[rows])
             at += w.shape[1]
             value = unit.gather(unit.values, group, unit.parity + 2 * high)
             own = own + jnp.dot(w, value, preferred_element_type=jnp.float32)
-        lanes = None
-        for (first, last), part in sums.items():
-            if not first <= rows.start < last:
-                continue
-            if last - first == 256:
-                part = part[rows]
-            lanes = part if lanes is None else lanes + part
+            lanes = lanes + part
+            yield
         result.append((lanes, own))
-    return result
 
 
 def biases(meta_ref):
@@ -191,9 +187,43 @@
     return {kind: jnp.where(inside, 0.0, -1e30).astype(jnp.float32) for kind, inside in usable.items()}
 
 
+def units_of(meta_ref, odd, keys, values):
+    return [Unit(meta_ref, i, parity, odd, keys, values) for i in range(4) for parity in range(2)]
+
+
+def attend(units, q_ref, s_refs, bias, state, emit, late=None):
+    before = lambda n: None if state is None else state[0][n]
+    tops = []
+    for _ in score(units[0], q_ref, s_refs[0], bias, before(0), tops):
+        pass
+    if late is not None:
+        late()
+    for n, unit in enumerate(units):
+        now, tops, result = tops, [], []
+        steps = [mix(unit, now, s_refs[n % 2], result)]
+        if n + 1 < len(units):
+            steps.insert(0, score(units[n + 1], q_ref, s_refs[(n + 1) % 2], bias, before(n + 1), tops))
+        for _ in itertools.zip_longest(*steps):
+            pass
+        for high, (lanes, mixed) in enumerate(result):
+            rows = slice(high * HD, (high + 1) * HD)
+            if state is not None:
+                carried = jnp.exp2((state[0][n, rows] - now[high]) * FACTOR)
+                lanes = lanes + state[1][n, rows] * carried
+                mixed = mixed + state[2][n, rows] * carried
+            emit(n, rows, high, now[high], lanes, mixed)
+
+
+def keep_in(top_ref, lanes_ref, total_ref):
+    def emit(n, rows, high, top, lanes, mixed):
+        top_ref[n, rows] = jnp.broadcast_to(top, (HD, HD))
+        lanes_ref[n, rows] = lanes
+        total_ref[n, rows] = mixed
+
+    return emit
+
+
 def attend_mine(meta_ref, q_ref, low, own_ref, high_ref, top_ref, lanes_ref, total_ref, s_even, s_odd):
-    bias = biases(meta_ref)
-
     def fetch(which):
         def of(i, d, at):
             n = place(i, d)[0]
@@ -201,22 +231,12 @@
 
         return of
 
-    units = [Unit(meta_ref, i, parity, 0, fetch(0), fetch(1)) for i in range(4) for parity in range(2)]
-    s_refs = (s_even, s_odd)
-    tops = score(units[0], q_ref, s_refs[0], bias)
-    for n, unit in enumerate(units):
-        now = tops
-        if n + 1 < len(units):
-            tops = score(units[n + 1], q_ref, s_refs[(n + 1) % 2], bias)
-        for high, (lanes, own) in enumerate(mix(unit, now, s_refs[n % 2])):
-            rows = slice(high * HD, (high + 1) * HD)
-            top_ref[n, rows] = jnp.broadcast_to(now[high], (HD, HD))
-            lanes_ref[n, rows] = lanes
-            total_ref[n, rows] = own
+    units = units_of(meta_ref, 0, fetch(0), fetch(1))
+    attend(units, q_ref, (s_even, s_odd), biases(meta_ref), None, keep_in(top_ref, lanes_ref, total_ref))
 
 
 def attend_theirs(
-    meta_ref, q_ref, top_ref, lanes_ref, total_ref, low, own_ref, high_ref, out_ref, k_ref, v_ref, s_even, s_odd, sems
+    meta_ref, q_ref, top_in, lanes_in, total_in, low, own_ref, high_ref, out_ref, k_ref, v_ref, s_even, s_odd, sems
 ):
     first = 1 - meta_ref[1]
     sources = ((low, first), (own_ref, first + 4), (high_ref, first + 8))
@@ -228,32 +248,25 @@
 
     k_copies = [load(src, 0, k_ref, slot, n) for n, (src, slot) in enumerate(sources)]
     v_copies = [load(src, 1, v_ref, slot, n + 3) for n, (src, slot) in enumerate(sources)]
-    bias = biases(meta_ref)
-
-    def keys(i, d, at):
-        return k_ref[(place(i, d)[0] + 1,) + at]
-
-    def values(i, d, at):
-        return v_ref[(place(i, d)[0] + 1,) + at]
-
-    units = [Unit(meta_ref, i, parity, 1, keys, values) for i in range(4) for parity in range(2)]
-    s_refs = (s_even, s_odd)
+
+    def fetch(ref):
+        return lambda i, d, at: ref[(place(i, d)[0] + 1,) + at]
+
+    def wait_values():
+        for made in v_copies:
+            made.wait()
+
+    units = units_of(meta_ref, 1, fetch(k_ref), fetch(v_ref))
+
+    def emit(n, rows, high, top, lanes, mixed):
+        row_sum = jnp.sum(lanes, axis=1, keepdims=True)
+        unit = units[n]
+        out_ref[unit.i, :, high, unit.parity] = (mixed / row_sum).astype(jnp.bfloat16).reshape(2, TOK, HD)
+
     for made in k_copies:
         made.wait()
-    tops = score(units[0], q_ref, s_refs[0], bias, top_ref[0])
-    for made in v_copies:
-        made.wait()
-    for n, unit in enumerate(units):
-        now = tops
-        if n + 1 < len(units):
-            tops = score(units[n + 1], q_ref, s_refs[(n + 1) % 2], bias, top_ref[n + 1])
-        for high, (lanes, mixed) in enumerate(mix(unit, now, s_refs[n % 2])):
-            rows = slice(high * HD, (high + 1) * HD)
-            carried = jnp.exp2((top_ref[n, rows] - now[high]) * FACTOR)
-            lanes = lanes + lanes_ref[n, rows] * carried
-            mixed = mixed + total_ref[n, rows] * carried
-            row_sum = jnp.sum(lanes, axis=1, keepdims=True)
-            out_ref[unit.i, :, high, unit.parity] = (mixed / row_sum).astype(jnp.bfloat16).reshape(2, TOK, HD)
+    state = (top_in, lanes_in, total_in)
+    attend(units, q_ref, (s_even, s_odd), biases(meta_ref), state, emit, wait_values)
 
 
 def side_by_side(x_ref, out_ref):
@@ -276,12 +289,6 @@
 
 def local(queries, keys, values, q_gain, k_gain, block_offset):
     half = jnp.bfloat16
-    z = lax.axis_index("z")
-    core = lax.axis_index("c")
-    frame = lax.dynamic_slice_in_dim(block_offset.reshape(8, 4, 2, 6), z, 1, 0)
-    table = lax.dynamic_slice_in_dim(frame, core, 1, 2).reshape(24)
-    meta = jnp.concatenate([jnp.stack([z, core]).astype(jnp.int32), table])
-
     tokens = pltpu.VMEM((TOK, HEADS * HD), half)
     kv = call(
         prepare_kv,
@@ -290,8 +297,18 @@
         scratch=[tokens, tokens, pltpu.VMEM((1, HEADS * HD), jnp.float32), pltpu.SemaphoreType.DMA((3,))],
         limit=PREPARE_LIMIT,
     )(keys, values, k_gain.reshape(1, -1))
-    queries, kv = lax.optimization_barrier((queries, kv))
-    q = call(prepare_q, jax.ShapeDtypeStruct((SLOTS, TOK, HD), half), [WHOLE] * 2)(queries, q_gain.reshape(1, -1))
+    queries, block_offset, kv = lax.optimization_barrier((queries, block_offset, kv))
+    z = lax.axis_index("z")
+    core = lax.axis_index("c")
+    frame = lax.dynamic_slice_in_dim(block_offset.reshape(8, 4, 2, 6), z, 1, 0)
+    table = lax.dynamic_slice_in_dim(frame, core, 1, 2).reshape(24)
+    meta = jnp.concatenate([jnp.stack([z, core]).astype(jnp.int32), table])
+    q, meta = call(
+        prepare_q,
+        [jax.ShapeDtypeStruct((SLOTS, TOK, HD), half), jax.ShapeDtypeStruct((META,), jnp.int32)],
+        [WHOLE] * 2 + [TABLE],
+        out_specs=[WHOLE, TABLE],
+    )(queries, q_gain.reshape(1, -1), meta)
     kv = exchange(kv)
     q, kv = lax.optimization_barrier((q, kv))
     blocks = (4, 2, 2, 2, TOK, HD)
@@ -304,14 +321,13 @@
     theirs = lax.ppermute(mine, "c", swap)
     their_low = lax.ppermute(low, "c", swap)
     their_high = lax.ppermute(high, "c", swap)
-
-    state = [jax.ShapeDtypeStruct((8, 256, HD), jnp.float32)] * 3
+    scores = lambda columns: [pltpu.VMEM((256, columns), jnp.float32)] * 2
     state = call(
         attend_mine,
-        state,
+        [jax.ShapeDtypeStruct((8, 256, HD), jnp.float32)] * 3,
         [TABLE] + [WHOLE] * 4,
         flops=4 * 4 * 1536 * 512 * HD,
-        scratch=[pltpu.VMEM((256, 1536), jnp.float32)] * 2,
+        scratch=scores(1536),
     )(meta, q, low, mine, high)
     kept = pltpu.VMEM((13, 2, 2, 2, TOK, HD), half)
     out = call(
@@ -319,7 +335,7 @@
         jax.ShapeDtypeStruct(blocks, half),
         [TABLE] + [WHOLE] * 4 + [ANYWHERE] * 3,
         flops=4 * 4 * 2048 * 512 * HD,
-        scratch=[kept, kept] + [pltpu.VMEM((256, 2048), jnp.float32)] * 2 + [pltpu.SemaphoreType.DMA((6,))],
+        scratch=[kept, kept] + scores(2048) + [pltpu.SemaphoreType.DMA((6,))],
     )(meta, q, *state, their_low, theirs, their_high)
     back = exchange(out.reshape(SLOTS, TOK, HD))
     return call(side_by_side, jax.ShapeDtypeStruct((TOK, HEADS * HD), half), [WHOLE])(back)

time: 115 us -> 116 us (level)
  Pallas kernels: 17.7 us -> 20.4 us
  waiting for transfers between devices: 42.2 us -> 40 us
    all_to_all x2, waiting for transfers between devices: 27.5 us -> 25.3 us  [exchange(): lax.all_to_all(x, ('x', 'y'), split_axis=0, concat_axis=0, tiled=True)]
    pallas_call x2, Pallas kernels: 6.49 us -> 8.34 us  [the longest x1 6.78 us: local(): call(attend_mine, [jax.ShapeDtypeStruct((8, 256, HD), jnp.float32)] * 3,...]
  transfers between devices with their start and end apart: 7 -> 7, of which waited for: 3 -> 3; matrix products, arithmetic and copies ran while one was open for 0% -> 0% of each run, Pallas kernels for 6% -> 7%
where the time goes in v2:
time: 116 us
  waiting for transfers between devices  40 us (34%)
  starting transfers between devices  28.6 us (25%)
  blocking collectives  25 us (22%)
  Pallas kernels  20.4 us (18%)
  local copies, waits for them, and re-layouts  1.55 us (1%)
    all_to_all x2, waiting for transfers between devices, exchange(): lax.all_to_all(x, ('x', 'y'), split_axis=0, concat_axis=0, tiled=True)  25.3 us
    all_to_all x1, blocking collectives, exchange(): lax.all_to_all(x, ('x', 'y'), split_axis=0, concat_axis=0, tiled=True)  25 us
    all_to_all x2, starting transfers between devices, exchange(): lax.all_to_all(x, ('x', 'y'), split_axis=0, concat_axis=0, tiled=True)  15.5 us
    ppermute x1, waiting for transfers between devices, local(): low = lax.ppermute(mine, 'z', [(n, n + 1) for n in range(7)])  11.2 us
    pallas_call x1, Pallas kernels, local(): call(attend_theirs, jax.ShapeDtypeStruct(blocks, half), [TABLE] + [WHOLE]...  9 us
    pallas_call x1, Pallas kernels, local(): call(attend_mine, [jax.ShapeDtypeStruct((8, 256, HD), jnp.float32)] * 3,...  6.78 us
    ppermute x1, starting transfers between devices, local(): low = lax.ppermute(mine, 'z', [(n, n + 1) for n in range(7)])  5.48 us
    ppermute x1, waiting for transfers between devices, local(): high = lax.ppermute(mine, 'z', [(n + 1, n) for n in range(7)])  3.52 us
  transfers between devices with their start and end apart: 7, of which 3 were waited for; matrix products, arithmetic and copies ran while one was open for 0% of the time, Pallas kernels for 7%

profile of v2, /device:TPU:200, one launch (start us, length us, event | category | flops | bytes accessed | tf_op | source)
XLA Modules:
  0.0 115.8 jit_solution(17919226231191954520)
XLA Ops:
  0.0 2.3 %shard_map.64 = bf16[32,2,64,128]{3,2,1,0:T(8,128)(2,1)} custom-call(bf16[64,3072]{1,0:T(8,128)(2,1)} %k_hbm.1, bf16[64,3072]{1,0:T(8,128)(2,1)} %v_hbm.1, f32[1,3072]{1,0:T(1,128)} %bitcast.19), custom_call_target="tpu_custom_call" | custom-call | bytes 4194304 | tf_op jit(solution)/shard_map/pallas_call | solution.py:293
  2.3 0.0 copy-start
  2.3 10.3 %all-to-all-start = ((bf16[32,2,64,128]{3,2,1,0:T(8,128)(2,1)}), bf16[32,2,64,128]{3,2,1,0:T(8,128)(2,1)S(1)}, u32[]{:S(2)}, u32[]{:S(2)}) async-start(bf16[32,2,64,128]{3,2,1,0:T(8,128)(2,1)} %shard_map.64), calls=%async_computation | async-start | bytes 2097152 | tf_op jit(solution)/shard_map/all_to_all | solution.py:287
  12.6 0.0 copy-start.2
  12.6 0.7 copy-done.2
  13.3 0.2 reshape.23
  13.5 0.1 constant_dynamic-slice_fusion
  13.6 0.0 copy-start.1
  13.6 0.1 copy.8
  13.7 0.1 reshape.24
  13.8 0.1 pad_add_fusion.meta_ref
  13.8 0.0 copy-done
  13.9 0.4 copy-done.1
  14.3 1.6 %shard_map.65 = (bf16[32,64,128]{2,1,0:T(8,128)(2,1)}, s32[26]{0:T(128)S(1)}) custom-call(bf16[64,3072]{1,0:T(8,128)(2,1)S(1)} %copy-done, f32[1,3072]{1,0:T(1,128)S(1)} %bitcast.18, s32[26]{0:T(128)S(1)} %pad_add_fusion.meta_ref), custom_call_target="tpu_custom_call" | custom-call | bytes 4194304 | tf_op jit(solution)/shard_map/pallas_call | solution.py:306
  15.8 25.3 %all-to-all-done = bf16[32,2,64,128]{3,2,1,0:T(8,128)(2,1)S(1)} async-done(((bf16[32,2,64,128]{3,2,1,0:T(8,128)(2,1)}), bf16[32,2,64,128]{3,2,1,0:T(8,128)(2,1)S(1)}, u32[]{:S(2)}, u32[]{:S(2)}) %all-to-all-start) | async-done | bytes 1048608 | tf_op jit(solution)/shard_map/all_to_all | solution.py:287
  41.1 5.5 %collective-permute-start = (bf16[4,2,2,2,2,64,128]{6,5,4,3,2,1,0:T(8,128)(2,1)S(1)}, bf16[4,2,2,2,2,64,128]{6,5,4,3,2,1,0:T(8,128)(2,1)S(1)}, u32[]{:S(2)}, u32[]{:S(2)}) collective-permute-start(bf16[4,2,2,2,2,64,128]{6,5,4,3,2,1,0:T(8,128)(2,1)S(1)} %bitcast.11), channel_id=1, source_target_pairs={{0,64},{64,128},{128,192},{192,256},{256,320},{320,384},{384,448},... | collective-permute-start | bytes 3145736 | tf_op jit(solution)/shard_map/ppermute | solution.py:319
  46.6 1.9 %collective-permute-start.1 = (bf16[4,2,2,2,2,64,128]{6,5,4,3,2,1,0:T(8,128)(2,1)S(1)}, bf16[4,2,2,2,2,64,128]{6,5,4,3,2,1,0:T(8,128)(2,1)}, u32[]{:S(2)}, u32[]{:S(2)}) collective-permute-start(bf16[4,2,2,2,2,64,128]{6,5,4,3,2,1,0:T(8,128)(2,1)S(1)} %bitcast.12), channel_id=1, source_target_pairs={{64,0},{128,64},{192,128},{256,192},{320,256},{384,320},{448,384},... | collective-permute-start | bytes 3145736 | tf_op jit(solution)/shard_map/ppermute | solution.py:320
  48.6 5.2 %all-to-all-start.1 = ((bf16[32,64,128]{2,1,0:T(8,128)(2,1)}), bf16[32,64,128]{2,1,0:T(8,128)(2,1)S(1)}, u32[]{:S(2)}, u32[]{:S(2)}) async-start(bf16[32,64,128]{2,1,0:T(8,128)(2,1)} %get-tuple-element.20), calls=%async_computation.1 | async-start | bytes 1048576 | tf_op jit(solution)/shard_map/all_to_all | solution.py:287
  53.8 1.9 %collective-permute-start.3 = (bf16[4,2,2,2,2,64,128]{6,5,4,3,2,1,0:T(8,128)(2,1)S(1)}, bf16[4,2,2,2,2,64,128]{6,5,4,3,2,1,0:T(8,128)(2,1)}, u32[]{:S(2)}, u32[]{:S(2)}) collective-permute-start(bf16[4,2,2,2,2,64,128]{6,5,4,3,2,1,0:T(8,128)(2,1)S(1)} %bitcast.13), channel_id=1, source_target_pairs={{0,8},{8,0},{1,9},{9,1},{2,10},{10,2},{3,11},{11,3},{4,12},{12,4},... | collective-permute-start | bytes 3145736 | tf_op jit(solution)/shard_map/ppermute | solution.py:321
  55.7 11.2 %collective-permute-done.low = bf16[4,2,2,2,2,64,128]{6,5,4,3,2,1,0:T(8,128)(2,1)S(1)} collective-permute-done((bf16[4,2,2,2,2,64,128]{6,5,4,3,2,1,0:T(8,128)(2,1)S(1)}, bf16[4,2,2,2,2,64,128]{6,5,4,3,2,1,0:T(8,128)(2,1)S(1)}, u32[]{:S(2)}, u32[]{:S(2)}) %collective-permute-start) | collective-permute-done | bytes 1048608 | tf_op jit(solution)/shard_map/ppermute | solution.py:319
  66.9 1.9 %collective-permute-start.2 = (bf16[4,2,2,2,2,64,128]{6,5,4,3,2,1,0:T(8,128)(2,1)S(1)}, bf16[4,2,2,2,2,64,128]{6,5,4,3,2,1,0:T(8,128)(2,1)}, u32[]{:S(2)}, u32[]{:S(2)}) collective-permute-start(bf16[4,2,2,2,2,64,128]{6,5,4,3,2,1,0:T(8,128)(2,1)S(1)} %collective-permute-done.low), channel_id=1, source_target_pairs={{0,8},{8,0},{1,9},{9,1},{2,10},{10,2},{3,11},{11,3},{4,12},{12,4},... | collective-permute-start | bytes 3145736 | tf_op jit(solution)/shard_map/ppermute | solution.py:322
  68.8 3.5 %collective-permute-done.1.high_ref = bf16[4,2,2,2,2,64,128]{6,5,4,3,2,1,0:T(8,128)(2,1)} collective-permute-done((bf16[4,2,2,2,2,64,128]{6,5,4,3,2,1,0:T(8,128)(2,1)S(1)}, bf16[4,2,2,2,2,64,128]{6,5,4,3,2,1,0:T(8,128)(2,1)}, u32[]{:S(2)}, u32[]{:S(2)}) %collective-permute-start.1) | collective-permute-done | bytes 1048608 | tf_op jit(solution)/shard_map/ppermute | solution.py:320
  72.3 1.9 %collective-permute-start.4 = (bf16[4,2,2,2,2,64,128]{6,5,4,3,2,1,0:T(8,128)(2,1)}, bf16[4,2,2,2,2,64,128]{6,5,4,3,2,1,0:T(8,128)(2,1)}, u32[]{:S(2)}, u32[]{:S(2)}) collective-permute-start(bf16[4,2,2,2,2,64,128]{6,5,4,3,2,1,0:T(8,128)(2,1)} %collective-permute-done.1.high_ref), channel_id=1, source_target_pairs={{0,8},{8,0},{1,9},{9,1},{2,10},{10,2},{3,11},{11,3},{4,12},{12,4},... | collective-permute-start | bytes 3145736 | tf_op jit(solution)/shard_map/ppermute | solution.py:323
  74.2 0.0 all-to-all-done.1
  74.2 6.8 %shard_map.66 = (f32[8,256,128]{2,1,0:T(8,128)S(1)}, f32[8,256,128]{2,1,0:T(8,128)S(1)}, f32[8,256,128]{2,1,0:T(8,128)S(1)}) custom-call(s32[26]{0:T(128)S(1)} %get-tuple-element.17.meta_ref, bf16[4,2,2,2,64,128]{5,4,3,2,1,0:T(8,128)(2,1)S(1)} %bitcast.15, bf16[4,2,2,2,2,64,128]{6,5,4,3,2,1,0:T(8,128)(2,1)S(1)} %collective-permute-done.low, ...), custom_call_target="tpu_custom_call" | custom-call | flops 1610612736 | bytes 4194304 | tf_op jit(solution)/shard_map/pallas_call | solution.py:325
  81.0 0.0 collective-permute-done.3.own_ref
  81.0 0.0 collective-permute-done.2.low
  81.0 0.0 collective-permute-done.4.high_ref
  81.0 9.0 %shard_map.67 = bf16[4,2,2,2,64,128]{5,4,3,2,1,0:T(8,128)(2,1)S(1)} custom-call(s32[26]{0:T(128)S(1)} %get-tuple-element.17.meta_ref, bf16[4,2,2,2,64,128]{5,4,3,2,1,0:T(8,128)(2,1)S(1)} %bitcast.16, f32[8,256,128]{2,1,0:T(8,128)S(1)} %get-tuple-element.22.top_in, f32[8,256,128]{2,1,0:T(8,128)S(1)} %get-tuple-element.23.lanes_in, ...), custom_call_target="tpu_custom_call" | custom-call | flops 2147483648 | bytes 4194304 | tf_op jit(solution)/shard_map/pallas_call | solution.py:333
  90.0 25.0 %all_to_all.15.x_ref = bf16[32,64,128]{2,1,0:T(8,128)(2,1)S(1)} all-to-all(bf16[32,64,128]{2,1,0:T(8,128)(2,1)S(1)} %bitcast.17), channel_id=1, replica_groups=mesh['z'=8,'x'=4,'c'=2,'y'=8] {'x','y'}, dimensions={0} | all-to-all | bytes 1048576 | tf_op jit(solution)/shard_map/all_to_all | solution.py:287
  115.0 0.8 shard_map.68
Async XLA Ops:
  2.3 11.6 %copy-start = (bf16[64,3072]{1,0:T(8,128)(2,1)S(1)}, bf16[64,3072]{1,0:T(8,128)(2,1)}, u32[]{:S(2)}) copy-start(bf16[64,3072]{1,0:T(8,128)(2,1)} %q_ref) | copy-start | bytes 1179652
  2.3 38.8 %all-to-all-start = ((bf16[32,2,64,128]{3,2,1,0:T(8,128)(2,1)}), bf16[32,2,64,128]{3,2,1,0:T(8,128)(2,1)S(1)}, u32[]{:S(2)}, u32[]{:S(2)}) async-start(bf16[32,2,64,128]{3,2,1,0:T(8,128)(2,1)} %shard_map.64), calls=%async_computation | async-start | bytes 2097152 | tf_op jit(solution)/shard_map/all_to_all | solution.py:287
  12.6 0.7 copy-start.2
  13.6 0.7 copy-start.1
  41.1 25.7 %collective-permute-start = (bf16[4,2,2,2,2,64,128]{6,5,4,3,2,1,0:T(8,128)(2,1)S(1)}, bf16[4,2,2,2,2,64,128]{6,5,4,3,2,1,0:T(8,128)(2,1)S(1)}, u32[]{:S(2)}, u32[]{:S(2)}) collective-permute-start(bf16[4,2,2,2,2,64,128]{6,5,4,3,2,1,0:T(8,128)(2,1)S(1)} %bitcast.11), channel_id=1, source_target_pairs={{0,64},{64,128},{128,192},{192,256},{256,320},{320,384},{384,448},... | collective-permute-start | bytes 3145736 | tf_op jit(solution)/shard_map/ppermute | solution.py:319
  46.6 25.7 %collective-permute-start.1 = (bf16[4,2,2,2,2,64,128]{6,5,4,3,2,1,0:T(8,128)(2,1)S(1)}, bf16[4,2,2,2,2,64,128]{6,5,4,3,2,1,0:T(8,128)(2,1)}, u32[]{:S(2)}, u32[]{:S(2)}) collective-permute-start(bf16[4,2,2,2,2,64,128]{6,5,4,3,2,1,0:T(8,128)(2,1)S(1)} %bitcast.12), channel_id=1, source_target_pairs={{64,0},{128,64},{192,128},{256,192},{320,256},{384,320},{448,384},... | collective-permute-start | bytes 3145736 | tf_op jit(solution)/shard_map/ppermute | solution.py:320
  48.6 25.6 %all-to-all-start.1 = ((bf16[32,64,128]{2,1,0:T(8,128)(2,1)}), bf16[32,64,128]{2,1,0:T(8,128)(2,1)S(1)}, u32[]{:S(2)}, u32[]{:S(2)}) async-start(bf16[32,64,128]{2,1,0:T(8,128)(2,1)} %get-tuple-element.20), calls=%async_computation.1 | async-start | bytes 1048576 | tf_op jit(solution)/shard_map/all_to_all | solution.py:287
  53.8 27.2 %collective-permute-start.3 = (bf16[4,2,2,2,2,64,128]{6,5,4,3,2,1,0:T(8,128)(2,1)S(1)}, bf16[4,2,2,2,2,64,128]{6,5,4,3,2,1,0:T(8,128)(2,1)}, u32[]{:S(2)}, u32[]{:S(2)}) collective-permute-start(bf16[4,2,2,2,2,64,128]{6,5,4,3,2,1,0:T(8,128)(2,1)S(1)} %bitcast.13), channel_id=1, source_target_pairs={{0,8},{8,0},{1,9},{9,1},{2,10},{10,2},{3,11},{11,3},{4,12},{12,4},... | collective-permute-start | bytes 3145736 | tf_op jit(solution)/shard_map/ppermute | solution.py:321
  66.9 14.2 %collective-permute-start.2 = (bf16[4,2,2,2,2,64,128]{6,5,4,3,2,1,0:T(8,128)(2,1)S(1)}, bf16[4,2,2,2,2,64,128]{6,5,4,3,2,1,0:T(8,128)(2,1)}, u32[]{:S(2)}, u32[]{:S(2)}) collective-permute-start(bf16[4,2,2,2,2,64,128]{6,5,4,3,2,1,0:T(8,128)(2,1)S(1)} %collective-permute-done.low), channel_id=1, source_target_pairs={{0,8},{8,0},{1,9},{9,1},{2,10},{10,2},{3,11},{11,3},{4,12},{12,4},... | collective-permute-start | bytes 3145736 | tf_op jit(solution)/shard_map/ppermute | solution.py:322
  72.3 8.7 %collective-permute-start.4 = (bf16[4,2,2,2,2,64,128]{6,5,4,3,2,1,0:T(8,128)(2,1)}, bf16[4,2,2,2,2,64,128]{6,5,4,3,2,1,0:T(8,128)(2,1)}, u32[]{:S(2)}, u32[]{:S(2)}) collective-permute-start(bf16[4,2,2,2,2,64,128]{6,5,4,3,2,1,0:T(8,128)(2,1)} %collective-permute-done.1.high_ref), channel_id=1, source_target_pairs={{0,8},{8,0},{1,9},{9,1},{2,10},{10,2},{3,11},{11,3},{4,12},{12,4},... | collective-permute-start | bytes 3145736 | tf_op jit(solution)/shard_map/ppermute | solution.py:323

commit v3 on v1

--- a/solution.py
+++ b/solution.py
@@ -21,6 +21,9 @@
 ANYWHERE = pl.BlockSpec(memory_space=pl.ANY)
 
 
+THEIRS = 13
+OWN_FLOPS = 40 * 8704 * 512 * HD
+FRAMES = 25
 DISTANCES = (0, 1, -1, 2, -2, 3, -3, 4, -4, 6, -6, 5, -5, 7, -7)
 
 
@@ -69,17 +72,17 @@
         n = 4 + i + d // 2
         return n, "low" if n < 4 else "high" if n >= 8 else None
     n = 4 + i + (d - 1) // 2
-    return n, "low" if n < 3 else "edge_low" if n == 3 else "high" if n >= 8 else "edge_high" if n == 7 else None
+    return THEIRS + n, "low" if n < 3 else "edge_low" if n == 3 else "high" if n >= 8 else "edge_high" if n == 7 else None
 
 
 class Unit:
-    def __init__(self, meta_ref, i, parity, odd, keys, values):
+    def __init__(self, meta_ref, i, parity, inside, keys, values):
         self.i = i
         self.parity = parity
         self.offs = [[meta_ref[2 + (i * 3 + level) * 2 + side] for side in range(2)] for level in range(3)]
         self.keys = keys
         self.values = values
-        used = [d for d in DISTANCES if d % 2 == odd]
+        used = [d for d in DISTANCES if (place(i, d)[1] is None) == inside]
         self.both = []
         self.far = []
         for size, groups in ((512, self.both), (256, self.both), (128, self.far)):
@@ -108,17 +111,16 @@
 def store_scores(unit, q, group, cls, s_ref, rows, start, bias):
     key = unit.gather(unit.keys, group, cls)
     s = lax.dot_general(q, key, (((1,), (1,)), ((), ())), preferred_element_type=jnp.float32)
-    size = width(group[0])
-    parts = [s[:, m * size : (m + 1) * size] for m in range(len(group))]
-    for m, d in enumerate(group):
-        kind = place(unit.i, d)[1]
-        parts[m] = parts[m] if kind is None else parts[m] + bias[kind]
-    s = jnp.concatenate(parts, axis=1)
+    if bias is not None:
+        size = width(group[0])
+        s = jnp.concatenate(
+            [s[:, m * size : (m + 1) * size] + bias[place(unit.i, d)[1]] for m, d in enumerate(group)], axis=1
+        )
     s_ref[rows, start : start + key.shape[0]] = s
     return lane_fold(jnp.maximum, s), start + key.shape[0]
 
 
-def score(unit, q_ref, s_ref, bias, before=None):
+def score(unit, q_ref, s_ref, before=None, bias=None):
     q = [unit.q(q_ref, high) for high in range(2)]
     both = jnp.concatenate(q, axis=0)
     top = before
@@ -179,35 +181,24 @@
     return result
 
 
-def biases(meta_ref):
-    z = meta_ref[0]
+def attend_own(meta_ref, q_ref, mine_ref, theirs_ref, top_ref, lanes_ref, total_ref, s_even, s_odd):
     core = meta_ref[1]
-    usable = {
-        "low": z > 0,
-        "edge_low": (z > 0) | (core == 1),
-        "edge_high": (z < 7) | (core == 0),
-        "high": z < 7,
-    }
-    return {kind: jnp.where(inside, 0.0, -1e30).astype(jnp.float32) for kind, inside in usable.items()}
-
-
-def attend_mine(meta_ref, q_ref, low, own_ref, high_ref, top_ref, lanes_ref, total_ref, s_even, s_odd):
-    bias = biases(meta_ref)
 
     def fetch(which):
         def of(i, d, at):
             n = place(i, d)[0]
-            return (low, own_ref, high_ref)[n // 4][(n % 4,) + at + (which,)]
+            ref, n = (mine_ref, n - 4) if d % 2 == 0 else (theirs_ref, n - THEIRS - 4 + core)
+            return ref[(n,) + at + (which,)]
 
         return of
 
-    units = [Unit(meta_ref, i, parity, 0, fetch(0), fetch(1)) for i in range(4) for parity in range(2)]
+    units = [Unit(meta_ref, i, parity, True, fetch(0), fetch(1)) for i in range(4) for parity in range(2)]
     s_refs = (s_even, s_odd)
-    tops = score(units[0], q_ref, s_refs[0], bias)
+    tops = score(units[0], q_ref, s_refs[0])
     for n, unit in enumerate(units):
         now = tops
         if n + 1 < len(units):
-            tops = score(units[n + 1], q_ref, s_refs[(n + 1) % 2], bias)
+            tops = score(units[n + 1], q_ref, s_refs[(n + 1) % 2])
         for high, (lanes, own) in enumerate(mix(unit, now, s_refs[n % 2])):
             rows = slice(high * HD, (high + 1) * HD)
             top_ref[n, rows] = jnp.broadcast_to(now[high], (HD, HD))
@@ -215,11 +206,14 @@
             total_ref[n, rows] = own
 
 
-def attend_theirs(
-    meta_ref, q_ref, top_ref, lanes_ref, total_ref, low, own_ref, high_ref, out_ref, k_ref, v_ref, s_even, s_odd, sems
+def attend_rest(
+    meta_ref, q_ref, top_ref, lanes_ref, total_ref, low, high_ref, their_own, their_low, their_high,
+    out_ref, k_ref, v_ref, s_even, s_odd, sems,
 ):
-    first = 1 - meta_ref[1]
-    sources = ((low, first), (own_ref, first + 4), (high_ref, first + 8))
+    z = meta_ref[0]
+    core = meta_ref[1]
+    sources = ((low, 0), (high_ref, 8), (their_low, THEIRS - core), (their_own, THEIRS - core + 4),
+               (their_high, THEIRS - core + 8))
 
     def load(src, which, ref, slot, n):
         made = pltpu.make_async_copy(src.at[:, :, :, :, which], ref.at[pl.ds(slot, 4)], sems.at[n])
@@ -227,26 +221,33 @@
         return made
 
     k_copies = [load(src, 0, k_ref, slot, n) for n, (src, slot) in enumerate(sources)]
-    v_copies = [load(src, 1, v_ref, slot, n + 3) for n, (src, slot) in enumerate(sources)]
-    bias = biases(meta_ref)
+    v_copies = [load(src, 1, v_ref, slot, n + 5) for n, (src, slot) in enumerate(sources)]
+    bias = {}
+    for kind, usable in (
+        ("low", z > 0),
+        ("edge_low", (z > 0) | (core == 1)),
+        ("edge_high", (z < 7) | (core == 0)),
+        ("high", z < 7),
+    ):
+        bias[kind] = jnp.where(usable, 0.0, -1e30).astype(jnp.float32)
 
     def keys(i, d, at):
-        return k_ref[(place(i, d)[0] + 1,) + at]
+        return k_ref[(place(i, d)[0],) + at]
 
     def values(i, d, at):
-        return v_ref[(place(i, d)[0] + 1,) + at]
-
-    units = [Unit(meta_ref, i, parity, 1, keys, values) for i in range(4) for parity in range(2)]
+        return v_ref[(place(i, d)[0],) + at]
+
+    units = [Unit(meta_ref, i, parity, False, keys, values) for i in range(4) for parity in range(2)]
     s_refs = (s_even, s_odd)
     for made in k_copies:
         made.wait()
-    tops = score(units[0], q_ref, s_refs[0], bias, top_ref[0])
+    tops = score(units[0], q_ref, s_refs[0], top_ref[0], bias)
     for made in v_copies:
         made.wait()
     for n, unit in enumerate(units):
         now = tops
         if n + 1 < len(units):
-            tops = score(units[n + 1], q_ref, s_refs[(n + 1) % 2], bias, top_ref[n + 1])
+            tops = score(units[n + 1], q_ref, s_refs[(n + 1) % 2], top_ref[n + 1], bias)
         for high, (lanes, mixed) in enumerate(mix(unit, now, s_refs[n % 2])):
             rows = slice(high * HD, (high + 1) * HD)
             carried = jnp.exp2((top_ref[n, rows] - now[high]) * FACTOR)
@@ -305,22 +306,17 @@
     their_low = lax.ppermute(low, "c", swap)
     their_high = lax.ppermute(high, "c", swap)
 
+    scores = [pltpu.VMEM((256, 2560), jnp.float32)] * 2
     state = [jax.ShapeDtypeStruct((8, 256, HD), jnp.float32)] * 3
-    state = call(
-        attend_mine,
-        state,
-        [TABLE] + [WHOLE] * 4,
-        flops=4 * 4 * 1536 * 512 * HD,
-        scratch=[pltpu.VMEM((256, 1536), jnp.float32)] * 2,
-    )(meta, q, low, mine, high)
-    kept = pltpu.VMEM((13, 2, 2, 2, TOK, HD), half)
+    state = call(attend_own, state, [TABLE] + [WHOLE] * 3, flops=OWN_FLOPS, scratch=scores)(meta, q, mine, theirs)
+    kept = pltpu.VMEM((FRAMES, 2, 2, 2, TOK, HD), half)
     out = call(
-        attend_theirs,
+        attend_rest,
         jax.ShapeDtypeStruct(blocks, half),
-        [TABLE] + [WHOLE] * 4 + [ANYWHERE] * 3,
-        flops=4 * 4 * 2048 * 512 * HD,
-        scratch=[kept, kept] + [pltpu.VMEM((256, 2048), jnp.float32)] * 2 + [pltpu.SemaphoreType.DMA((6,))],
-    )(meta, q, *state, their_low, theirs, their_high)
+        [TABLE] + [WHOLE] * 4 + [ANYWHERE] * 5,
+        flops=4 * 5632 * 512 * HD,
+        scratch=[kept, kept] + scores + [pltpu.SemaphoreType.DMA((10,))],
+    )(meta, q, *state, low, high, theirs, their_low, their_high)
     back = exchange(out.reshape(SLOTS, TOK, HD))
     return call(side_by_side, jax.ShapeDtypeStruct((TOK, HEADS * HD), half), [WHOLE])(back)
 

time: 115 us -> 116 us (level)
  transfers between devices with their start and end apart: 7 -> 7, of which waited for: 3 -> 3; matrix products, arithmetic and copies ran while one was open for 0% -> 0% of each run, Pallas kernels for 6% -> 7%
where the time goes in v3:
time: 116 us; the launch traced here: 115 us
  waiting for transfers between devices  41.2 us (36%)
  starting transfers between devices  28.7 us (25%)
  blocking collectives  25 us (22%)
  Pallas kernels  18.8 us (16%)
    all_to_all x2, waiting for transfers between devices, exchange(): lax.all_to_all(x, ('x', 'y'), split_axis=0, concat_axis=0, tiled=True)  27.6 us
    all_to_all x1, blocking collectives, exchange(): lax.all_to_all(x, ('x', 'y'), split_axis=0, concat_axis=0, tiled=True)  25 us
    all_to_all x2, starting transfers between devices, exchange(): lax.all_to_all(x, ('x', 'y'), split_axis=0, concat_axis=0, tiled=True)  15.6 us
    ppermute x1, waiting for transfers between devices, local(): low = lax.ppermute(mine, 'z', [(n, n + 1) for n in range(7)])  10.2 us
    pallas_call x1, Pallas kernels, local(): call(attend_own, state, [TABLE] + [WHOLE] * 3, flops=OWN_FLOPS, scratch=s...  7.49 us
    pallas_call x1, Pallas kernels, local(): call(attend_rest, jax.ShapeDtypeStruct(blocks, half), [TABLE] + [WHOLE] *...  7.12 us
    ppermute x1, starting transfers between devices, local(): low = lax.ppermute(mine, 'z', [(n, n + 1) for n in range(7)])  5.48 us
    ppermute x1, waiting for transfers between devices, local(): high = lax.ppermute(mine, 'z', [(n + 1, n) for n in range(7)])  3.41 us
  transfers between devices with their start and end apart: 7, of which 3 were waited for; matrix products, arithmetic and copies ran while one was open for 0% of the time, Pallas kernels for 7%

profile of v3, /device:TPU:200, one launch (start us, length us, event | category | flops | bytes accessed | tf_op | source)
XLA Modules:
  0.0 115.1 jit_solution(14861715006103917886)
XLA Ops:
  0.0 2.3 %shard_map.64 = bf16[32,2,64,128]{3,2,1,0:T(8,128)(2,1)} custom-call(bf16[64,3072]{1,0:T(8,128)(2,1)} %k_hbm.1, bf16[64,3072]{1,0:T(8,128)(2,1)} %v_hbm.1, f32[1,3072]{1,0:T(1,128)} %bitcast.15), custom_call_target="tpu_custom_call" | custom-call | bytes 4194304 | tf_op jit(solution)/shard_map/pallas_call | solution.py:287
  2.3 0.0 copy-start.1
  2.3 0.0 copy-start.2
  2.3 10.4 %all-to-all-start = ((bf16[32,2,64,128]{3,2,1,0:T(8,128)(2,1)}), bf16[32,2,64,128]{3,2,1,0:T(8,128)(2,1)}, u32[]{:S(2)}, u32[]{:S(2)}) async-start(bf16[32,2,64,128]{3,2,1,0:T(8,128)(2,1)} %shard_map.64), calls=%async_computation | async-start | bytes 2097152 | tf_op jit(solution)/shard_map/all_to_all | solution.py:275
  12.7 0.0 copy-done.1
  12.7 0.0 copy-done.2
  12.7 1.0 shard_map.65
  13.7 27.6 %all-to-all-done = bf16[32,2,64,128]{3,2,1,0:T(8,128)(2,1)} async-done(((bf16[32,2,64,128]{3,2,1,0:T(8,128)(2,1)}), bf16[32,2,64,128]{3,2,1,0:T(8,128)(2,1)}, u32[]{:S(2)}, u32[]{:S(2)}) %all-to-all-start) | async-done | bytes 1048608 | tf_op jit(solution)/shard_map/all_to_all | solution.py:275
  41.3 5.5 %collective-permute-start.1 = (bf16[4,2,2,2,2,64,128]{6,5,4,3,2,1,0:T(8,128)(2,1)}, bf16[4,2,2,2,2,64,128]{6,5,4,3,2,1,0:T(8,128)(2,1)S(1)}, u32[]{:S(2)}, u32[]{:S(2)}) collective-permute-start(bf16[4,2,2,2,2,64,128]{6,5,4,3,2,1,0:T(8,128)(2,1)} %bitcast.5.mine_ref), channel_id=1, source_target_pairs={{0,64},{64,128},{128,192},{192,256},{256,320},{320,384},{384,448},... | collective-permute-start | bytes 3145736 | tf_op jit(solution)/shard_map/ppermute | solution.py:303
  46.8 1.9 %collective-permute-start.2 = (bf16[4,2,2,2,2,64,128]{6,5,4,3,2,1,0:T(8,128)(2,1)}, bf16[4,2,2,2,2,64,128]{6,5,4,3,2,1,0:T(8,128)(2,1)}, u32[]{:S(2)}, u32[]{:S(2)}) collective-permute-start(bf16[4,2,2,2,2,64,128]{6,5,4,3,2,1,0:T(8,128)(2,1)} %bitcast.5.mine_ref), channel_id=1, source_target_pairs={{64,0},{128,64},{192,128},{256,192},{320,256},{384,320},{448,384},... | collective-permute-start | bytes 3145736 | tf_op jit(solution)/shard_map/ppermute | solution.py:304
  48.7 1.9 %collective-permute-start = (bf16[4,2,2,2,2,64,128]{6,5,4,3,2,1,0:T(8,128)(2,1)}, bf16[4,2,2,2,2,64,128]{6,5,4,3,2,1,0:T(8,128)(2,1)S(1)}, u32[]{:S(2)}, u32[]{:S(2)}) collective-permute-start(bf16[4,2,2,2,2,64,128]{6,5,4,3,2,1,0:T(8,128)(2,1)} %bitcast.5.mine_ref), channel_id=1, source_target_pairs={{0,8},{8,0},{1,9},{9,1},{2,10},{10,2},{3,11},{11,3},{4,12},{12,4},... | collective-permute-start | bytes 3145736 | tf_op jit(solution)/shard_map/ppermute | solution.py:305
  50.6 5.2 %all-to-all-start.1 = ((bf16[32,64,128]{2,1,0:T(8,128)(2,1)}), bf16[32,64,128]{2,1,0:T(8,128)(2,1)S(1)}, u32[]{:S(2)}, u32[]{:S(2)}) async-start(bf16[32,64,128]{2,1,0:T(8,128)(2,1)} %shard_map.65), calls=%async_computation.1 | async-start | bytes 1048576 | tf_op jit(solution)/shard_map/all_to_all | solution.py:275
  55.9 0.0 copy-start.3
  55.9 0.7 copy-done.3
  56.5 0.2 reshape.21
  56.7 0.1 constant_dynamic-slice_fusion
  56.8 0.1 copy.8
  56.9 0.1 reshape.22
  57.0 0.1 pad_add_fusion.meta_ref
  57.1 10.2 %collective-permute-done.1.low = bf16[4,2,2,2,2,64,128]{6,5,4,3,2,1,0:T(8,128)(2,1)S(1)} collective-permute-done((bf16[4,2,2,2,2,64,128]{6,5,4,3,2,1,0:T(8,128)(2,1)}, bf16[4,2,2,2,2,64,128]{6,5,4,3,2,1,0:T(8,128)(2,1)S(1)}, u32[]{:S(2)}, u32[]{:S(2)}) %collective-permute-start.1) | collective-permute-done | bytes 1048608 | tf_op jit(solution)/shard_map/ppermute | solution.py:303
  67.3 1.9 %collective-permute-start.3 = (bf16[4,2,2,2,2,64,128]{6,5,4,3,2,1,0:T(8,128)(2,1)S(1)}, bf16[4,2,2,2,2,64,128]{6,5,4,3,2,1,0:T(8,128)(2,1)}, u32[]{:S(2)}, u32[]{:S(2)}) collective-permute-start(bf16[4,2,2,2,2,64,128]{6,5,4,3,2,1,0:T(8,128)(2,1)S(1)} %collective-permute-done.1.low), channel_id=1, source_target_pairs={{0,8},{8,0},{1,9},{9,1},{2,10},{10,2},{3,11},{11,3},{4,12},{12,4},... | collective-permute-start | bytes 3145736 | tf_op jit(solution)/shard_map/ppermute | solution.py:306
  69.2 3.4 %collective-permute-done.2.high_ref = bf16[4,2,2,2,2,64,128]{6,5,4,3,2,1,0:T(8,128)(2,1)} collective-permute-done((bf16[4,2,2,2,2,64,128]{6,5,4,3,2,1,0:T(8,128)(2,1)}, bf16[4,2,2,2,2,64,128]{6,5,4,3,2,1,0:T(8,128)(2,1)}, u32[]{:S(2)}, u32[]{:S(2)}) %collective-permute-start.2) | collective-permute-done | bytes 1048608 | tf_op jit(solution)/shard_map/ppermute | solution.py:304
  72.7 1.9 %collective-permute-start.4 = (bf16[4,2,2,2,2,64,128]{6,5,4,3,2,1,0:T(8,128)(2,1)}, bf16[4,2,2,2,2,64,128]{6,5,4,3,2,1,0:T(8,128)(2,1)}, u32[]{:S(2)}, u32[]{:S(2)}) collective-permute-start(bf16[4,2,2,2,2,64,128]{6,5,4,3,2,1,0:T(8,128)(2,1)} %collective-permute-done.2.high_ref), channel_id=1, source_target_pairs={{0,8},{8,0},{1,9},{9,1},{2,10},{10,2},{3,11},{11,3},{4,12},{12,4},... | collective-permute-start | bytes 3145736 | tf_op jit(solution)/shard_map/ppermute | solution.py:307
  74.6 0.0 all-to-all-done.1
  74.6 0.0 collective-permute-done.theirs_ref.their_own
  74.6 0.0 copy-start
  74.6 7.5 %shard_map.66 = (f32[8,256,128]{2,1,0:T(8,128)S(1)}, f32[8,256,128]{2,1,0:T(8,128)S(1)}, f32[8,256,128]{2,1,0:T(8,128)S(1)}) custom-call(s32[26]{0:T(128)S(1)} %pad_add_fusion.meta_ref, bf16[4,2,2,2,64,128]{5,4,3,2,1,0:T(8,128)(2,1)S(1)} %bitcast.11, bf16[4,2,2,2,2,64,128]{6,5,4,3,2,1,0:T(8,128)(2,1)} %bitcast.5.mine_ref, ...), custom_call_target="tpu_custom_call" | custom-call | flops 22817013760 | bytes 4194304 | tf_op jit(solution)/shard_map/pallas_call | solution.py:311
  82.1 0.0 collective-permute-done.3.their_low
  82.1 0.0 collective-permute-done.4.their_high
  82.1 7.1 %shard_map.67 = bf16[4,2,2,2,64,128]{5,4,3,2,1,0:T(8,128)(2,1)S(1)} custom-call(s32[26]{0:T(128)S(1)} %pad_add_fusion.meta_ref, bf16[4,2,2,2,64,128]{5,4,3,2,1,0:T(8,128)(2,1)S(1)} %bitcast.12, f32[8,256,128]{2,1,0:T(8,128)S(1)} %get-tuple-element.16.top_ref, f32[8,256,128]{2,1,0:T(8,128)S(1)} %get-tuple-element.17.lanes_ref, ...), custom_call_target="tpu_custom_call" | custom-call | flops 1476395008 | bytes 4194304 | tf_op jit(solution)/shard_map/pallas_call | solution.py:313
  89.3 25.0 %all_to_all.15.x_ref = bf16[32,64,128]{2,1,0:T(8,128)(2,1)S(1)} all-to-all(bf16[32,64,128]{2,1,0:T(8,128)(2,1)S(1)} %bitcast.13), channel_id=1, replica_groups=mesh['z'=8,'x'=4,'c'=2,'y'=8] {'x','y'}, dimensions={0} | all-to-all | bytes 1048576 | tf_op jit(solution)/shard_map/all_to_all | solution.py:275
  114.2 0.8 shard_map.68
  (1 shorter events, 0.0 us)
Async XLA Ops:
  2.3 10.4 %copy-start.1 = (bf16[64,3072]{1,0:T(8,128)(2,1)S(1)}, bf16[64,3072]{1,0:T(8,128)(2,1)}, u32[]{:S(2)}) copy-start(bf16[64,3072]{1,0:T(8,128)(2,1)} %q_ref) | copy-start | bytes 1179652
  2.3 10.4 %copy-start.2 = (f32[3072]{0:T(1024)S(1)}, f32[3072]{0:T(1024)}, u32[]{:S(2)}) copy-start(f32[3072]{0:T(1024)} %param.9) | copy-start | bytes 36868
  2.3 39.0 %all-to-all-start = ((bf16[32,2,64,128]{3,2,1,0:T(8,128)(2,1)}), bf16[32,2,64,128]{3,2,1,0:T(8,128)(2,1)}, u32[]{:S(2)}, u32[]{:S(2)}) async-start(bf16[32,2,64,128]{3,2,1,0:T(8,128)(2,1)} %shard_map.64), calls=%async_computation | async-start | bytes 2097152 | tf_op jit(solution)/shard_map/all_to_all | solution.py:275
  41.3 26.0 %collective-permute-start.1 = (bf16[4,2,2,2,2,64,128]{6,5,4,3,2,1,0:T(8,128)(2,1)}, bf16[4,2,2,2,2,64,128]{6,5,4,3,2,1,0:T(8,128)(2,1)S(1)}, u32[]{:S(2)}, u32[]{:S(2)}) collective-permute-start(bf16[4,2,2,2,2,64,128]{6,5,4,3,2,1,0:T(8,128)(2,1)} %bitcast.5.mine_ref), channel_id=1, source_target_pairs={{0,64},{64,128},{128,192},{192,256},{256,320},{320,384},{384,448},... | collective-permute-start | bytes 3145736 | tf_op jit(solution)/shard_map/ppermute | solution.py:303
  46.8 25.9 %collective-permute-start.2 = (bf16[4,2,2,2,2,64,128]{6,5,4,3,2,1,0:T(8,128)(2,1)}, bf16[4,2,2,2,2,64,128]{6,5,4,3,2,1,0:T(8,128)(2,1)}, u32[]{:S(2)}, u32[]{:S(2)}) collective-permute-start(bf16[4,2,2,2,2,64,128]{6,5,4,3,2,1,0:T(8,128)(2,1)} %bitcast.5.mine_ref), channel_id=1, source_target_pairs={{64,0},{128,64},{192,128},{256,192},{320,256},{384,320},{448,384},... | collective-permute-start | bytes 3145736 | tf_op jit(solution)/shard_map/ppermute | solution.py:304
  48.7 25.9 %collective-permute-start = (bf16[4,2,2,2,2,64,128]{6,5,4,3,2,1,0:T(8,128)(2,1)}, bf16[4,2,2,2,2,64,128]{6,5,4,3,2,1,0:T(8,128)(2,1)S(1)}, u32[]{:S(2)}, u32[]{:S(2)}) collective-permute-start(bf16[4,2,2,2,2,64,128]{6,5,4,3,2,1,0:T(8,128)(2,1)} %bitcast.5.mine_ref), channel_id=1, source_target_pairs={{0,8},{8,0},{1,9},{9,1},{2,10},{10,2},{3,11},{11,3},{4,12},{12,4},... | collective-permute-start | bytes 3145736 | tf_op jit(solution)/shard_map/ppermute | solution.py:305
  50.6 23.9 %all-to-all-start.1 = ((bf16[32,64,128]{2,1,0:T(8,128)(2,1)}), bf16[32,64,128]{2,1,0:T(8,128)(2,1)S(1)}, u32[]{:S(2)}, u32[]{:S(2)}) async-start(bf16[32,64,128]{2,1,0:T(8,128)(2,1)} %shard_map.65), calls=%async_computation.1 | async-start | bytes 1048576 | tf_op jit(solution)/shard_map/all_to_all | solution.py:275
  55.9 0.7 copy-start.3
  67.3 14.8 %collective-permute-start.3 = (bf16[4,2,2,2,2,64,128]{6,5,4,3,2,1,0:T(8,128)(2,1)S(1)}, bf16[4,2,2,2,2,64,128]{6,5,4,3,2,1,0:T(8,128)(2,1)}, u32[]{:S(2)}, u32[]{:S(2)}) collective-permute-start(bf16[4,2,2,2,2,64,128]{6,5,4,3,2,1,0:T(8,128)(2,1)S(1)} %collective-permute-done.1.low), channel_id=1, source_target_pairs={{0,8},{8,0},{1,9},{9,1},{2,10},{10,2},{3,11},{11,3},{4,12},{12,4},... | collective-permute-start | bytes 3145736 | tf_op jit(solution)/shard_map/ppermute | solution.py:306
  72.7 9.5 %collective-permute-start.4 = (bf16[4,2,2,2,2,64,128]{6,5,4,3,2,1,0:T(8,128)(2,1)}, bf16[4,2,2,2,2,64,128]{6,5,4,3,2,1,0:T(8,128)(2,1)}, u32[]{:S(2)}, u32[]{:S(2)}) collective-permute-start(bf16[4,2,2,2,2,64,128]{6,5,4,3,2,1,0:T(8,128)(2,1)} %collective-permute-done.2.high_ref), channel_id=1, source_target_pairs={{0,8},{8,0},{1,9},{9,1},{2,10},{10,2},{3,11},{11,3},{4,12},{12,4},... | collective-permute-start | bytes 3145736 | tf_op jit(solution)/shard_map/ppermute | solution.py:307
  74.6 7.5 %copy-start = (bf16[4,2,2,2,2,64,128]{6,5,4,3,2,1,0:T(8,128)(2,1)}, bf16[4,2,2,2,2,64,128]{6,5,4,3,2,1,0:T(8,128)(2,1)S(1)}, u32[]{:S(2)}) copy-start(bf16[4,2,2,2,2,64,128]{6,5,4,3,2,1,0:T(8,128)(2,1)S(1)} %collective-permute-done.theirs_ref.their_own) | copy-start | bytes 3145732
